TPU v7x, 512 devices: a whole 4x8x8 slice. The times are simulated.
512 devices in a mesh: gx: 32 (over x, y), gy: 16 (over z, core).
Axes of the slice: x: 4, y: 8, z: 8, core: 2. Of those that a mesh axis runs over, the one named last changes fastest.
Arguments:
- positions: float32 [3, 1048576], P(None, ('gx', 'gy')), may hold values from 0 to 32, as said below
- density: float32 [1048576], P(('gx', 'gy')), may hold values from 0.5 to 4
- momentum: float32 [3, 1048576], P(None, ('gx', 'gy')), may hold values from -3 to 3
- field: float32 [3, 1048576], P(None, ('gx', 'gy')), may hold values from -3 to 3
- psi: float32 [1048576], P(('gx', 'gy')), may hold values from -3 to 3
- ohmic: float32 [1048576], P(('gx', 'gy')), may hold values from 0.05 to 20
- ambipolar: float32 [1048576], P(('gx', 'gy')), may hold values from 0.02 to 0.3
- ghost_index: int32 [557056], P(('gx', 'gy')), may hold values from 0 to 2047, as said below
- tile_i: int32 [32768], P(('gx', 'gy')), may hold values from 0 to 15, as said below
- tile_j: int32 [32768], P(('gx', 'gy')), may hold values from 0 to 24, as said below
- tile_count: int32 [512], P(('gx', 'gy')), may hold values from 16 to 64, as said below
Outputs:
- density_new: float32 [1048576], P(('gx', 'gy'))
- momentum_new: float32 [3, 1048576], P(None, ('gx', 'gy'))
- field_new: float32 [3, 1048576], P(None, ('gx', 'gy'))
- psi_new: float32 [1048576], P(('gx', 'gy'))
Inputs may be any that keep to these rules, and one draw needn't show every extreme that they name: `positions`: x lies in [ix, ix+1) and y in [iy, iy+1) for the owner (ix, iy); z lies in [0, 0.5). `ghost_index`: within one device the 1088 numbers are distinct. `tile_i`: a block of 128 local particles. `tile_j`: a block of 128 in the extended set; the pairs (tile_i, tile_j) of one device are distinct. `tile_count`: the devices of a dense region of three by three slabs use all 64 entries.
All inputs are finite; a program needn't handle non-finite values.
Results may differ from a plain program's by a relative error of at most 0.0003.
Values sent between devices are 32-bit elements; how exact they have to be, the bound alone decides.
A program may use at most 64 MiB of HBM per device.

v0:
```python
import math

import jax
import jax.numpy as jnp
from jax import lax
from jax.sharding import PartitionSpec as P

TILE = 128
SECTIONS = 4
GHOST_X = 320
GHOST_Y = 160
GHOST_C = 32
EXT_BLOCKS = 25


DIRECTIONS = [(-1, -1), (-1, 0), (-1, 1), (0, -1), (0, 1), (1, -1), (1, 0), (1, 1)]
courant = 0.3
damping = 0.5


def extended(array, sides, width):
    for axis, dim in sides:
        size, length = (lax.axis_size(axis), array.shape[dim])
        up = [(i, (i + 1) % size) for i in range(size - 1)]
        down = [(j, i) for i, j in up]
        last = lax.slice_in_dim(array, length - width, length, axis=dim)
        leading = lax.slice_in_dim(array, 0, width, axis=dim)
        before = lax.ppermute(last, axis, up)
        after = lax.ppermute(leading, axis, down)
        array = jnp.concatenate([before, array, after], axis=dim)
    return array


def ghost_sizes():
    return [GHOST_C, GHOST_X, GHOST_C, GHOST_Y, GHOST_Y, GHOST_C, GHOST_X, GHOST_C]


def ghost_offsets():
    sizes = ghost_sizes()
    starts = [0]
    for value in sizes[:-1]:
        starts.append(starts[-1] + value)
    return starts


def rkl_table(sections):
    wfirst = 4.0 / (sections * sections + sections - 2)
    bvals = [1.0 / 3.0, 1.0 / 3.0, 1.0 / 3.0] + [
        (j * j + j - 2) / (2.0 * j * (j + 1)) for j in range(3, sections + 1)
    ]
    first = bvals[1] * wfirst
    rows = []
    for j in range(2, sections + 1):
        mu_j = (2.0 * j - 1.0) / j * bvals[j] / bvals[j - 1]
        nu_j = -(j - 1.0) / j * bvals[j] / bvals[j - 2]
        mut_j = mu_j * wfirst
        rows.append((mu_j, nu_j, mut_j, -(1.0 - bvals[j - 1]) * mut_j))
    return (first, rows)


def kernel_tile(near, far):
    dist = (near[0][..., :, None] - far[0][..., None, :]) ** 2
    dist = dist + (near[1][..., :, None] - far[1][..., None, :]) ** 2
    dist = dist + (near[2][..., :, None] - far[2][..., None, :]) ** 2
    base = jnp.maximum(1.0 - 4.0 * dist, 0.0)
    return base * base


def flux_rows(ext, ch):
    posit = ext[0:3]
    live = ext[3]
    rho = ext[4]
    vel = ext[5:8]
    bfl = ext[8:11]
    cpsi = ext[11]
    speed = ext[12]
    mom = rho * vel
    ptot = rho + 0.5 * jnp.sum(bfl * bfl, axis=0)
    fluxes = []
    for d in range(3):
        rows_d = [mom[d]]
        for k in range(3):
            term = mom[k] * vel[d] - bfl[k] * bfl[d]
            rows_d.append(term + ptot if k == d else term)
        for k in range(3):
            term = vel[d] * bfl[k] - bfl[d] * vel[k]
            rows_d.append(term + cpsi if k == d else term)
        rows_d.append(ch * ch * bfl[d])
        fluxes.append(jnp.stack(rows_d))
    flux = jnp.stack(fluxes)
    state = jnp.concatenate([rho[None], mom, bfl, cpsi[None]], axis=0)
    gsum = posit[0] * flux[0] + posit[1] * flux[1] + posit[2] * flux[2]
    return jnp.concatenate(
        [live[None], posit, flux.reshape(24, -1), gsum, speed * state, speed[None], state], axis=0
    )


def hydro_rate(acc, local):
    count_n = acc[0]
    num = acc.shape[1]
    wflux = acc[4:28].reshape(3, 8, num)
    flux = local[4:28].reshape(3, 8, num)
    posit = local[1:4]
    speed = local[44]
    state = local[45:53]
    central = acc[28:36]
    for d in range(3):
        central = central + flux[d] * (acc[1 + d] - posit[d] * count_n) - posit[d] * wflux[d]
    dissip = speed * (acc[45:53] - state * count_n) + acc[36:44] - state * acc[44]
    return ((0.5 * dissip - 0.5 * central) / (1.0 + count_n), count_n)


def diffusion_rate(acc, bloc, etaloc, count_n):
    return 0.5 * (etaloc * (acc[0:3] - bloc * count_n) + acc[3:6] - bloc * acc[6]) / (1.0 + count_n)


def spread_ghosts(rows, ghost_index):
    sizes = ghost_sizes()
    starts = ghost_offsets()
    sends = [
        jnp.take(rows, ghost_index[starts[d] : starts[d] + sizes[d]], axis=1) for d in range(8)
    ]

    def toward(p, q):
        return sends[DIRECTIONS.index((p, q))]

    got = {}
    face_x = GHOST_X
    corner = GHOST_C
    face_y = GHOST_Y
    toward_low = jnp.concatenate([toward(-1, 0), toward(-1, -1), toward(-1, 1)], axis=1)
    toward_high = jnp.concatenate([toward(1, 0), toward(1, -1), toward(1, 1)], axis=1)
    along_x = extended(jnp.stack([toward_low, toward_high]), (("gx", 0),), 1)
    from_low = along_x[0]
    from_high = along_x[3]
    downward = jnp.concatenate(
        [
            toward(0, -1),
            from_low[:, face_x : face_x + corner],
            from_high[:, face_x : face_x + corner],
        ],
        axis=1,
    )
    upward = jnp.concatenate(
        [toward(0, 1), from_low[:, face_x + corner :], from_high[:, face_x + corner :]], axis=1
    )
    along_y = extended(jnp.stack([downward, upward]), (("gy", 0),), 1)
    from_below = along_y[0]
    from_above = along_y[3]
    got[-1, 0] = from_low[:, :face_x]
    got[1, 0] = from_high[:, :face_x]
    got[0, -1] = from_below[:, :face_y]
    got[0, 1] = from_above[:, :face_y]
    got[-1, -1] = from_below[:, face_y : face_y + corner]
    got[1, -1] = from_below[:, face_y + corner :]
    got[-1, 1] = from_above[:, face_y : face_y + corner]
    got[1, 1] = from_above[:, face_y + corner :]
    return jnp.concatenate([got[p, q] for p, q in DIRECTIONS], axis=1)


def extend(rows, extra):
    filler = jnp.zeros(
        (rows.shape[0], EXT_BLOCKS * TILE - rows.shape[1] - extra.shape[1]), jnp.float32
    )
    return jnp.concatenate([rows, extra, filler], axis=1)


def shards(
    positions,
    density,
    momentum,
    field,
    psi,
    ohmic,
    ambipolar,
    ghost_index,
    tile_i,
    tile_j,
    tile_count,
):
    nlocal = density.shape[0]
    nblocks = nlocal // TILE
    velocity = momentum / density
    speed = jnp.sqrt(1.0 + jnp.sum(field * field, axis=0) / density)
    fac = ambipolar / (density * jnp.sqrt(density))
    live = jnp.ones_like(density)
    core_rows = [positions, live[None], density[None], velocity, field, psi[None], speed[None]]
    payload = jnp.concatenate(core_rows, axis=0)
    ch = lax.pmax(jnp.max(speed), ("gx", "gy"))
    dt = courant / ch
    ghosts = spread_ghosts(payload, ghost_index)
    ext = extend(payload, ghosts)
    pos_blocks = ext[0:3].reshape(3, EXT_BLOCKS, TILE)
    qext = flux_rows(ext, ch)
    q_blocks = qext.reshape(qext.shape[0], EXT_BLOCKS, TILE)
    count = tile_count[0]
    tiles_total = tile_i.shape[0]
    batch = math.gcd(32, tiles_total)
    rounds = (count + batch - 1) // batch
    block_ids = jnp.arange(nblocks, dtype=jnp.int32)

    def batch_lists(offset):
        near_ids = lax.dynamic_slice_in_dim(tile_i, offset, batch, 0)
        far_ids = lax.dynamic_slice_in_dim(tile_j, offset, batch, 0)
        usable = offset + jnp.arange(batch, dtype=jnp.int32) < count
        onehot = ((near_ids[None, :] == block_ids[:, None]) & usable[None, :]).astype(jnp.float32)
        return (near_ids, far_ids, onehot)

    def fold_batch(acc, blocks, weight, far_ids, onehot):
        qsel = jnp.take(blocks, far_ids, axis=1)
        part = jnp.einsum(
            "rtb,tab->rta",
            qsel,
            weight,
            precision=lax.Precision.HIGHEST,
            preferred_element_type=jnp.float32,
        )
        return acc + jnp.einsum(
            "pt,rta->rpa",
            onehot,
            part,
            precision=lax.Precision.HIGHEST,
            preferred_element_type=jnp.float32,
        )

    def hydro_step(turn, carry):
        acc, stored = carry
        offset = (turn * batch).astype(jnp.int32)
        near_ids, far_ids, onehot = batch_lists(offset)
        near = jnp.take(pos_blocks, near_ids, axis=1)
        far = jnp.take(pos_blocks, far_ids, axis=1)
        weight = kernel_tile(near, far)
        stored = lax.dynamic_update_slice_in_dim(stored, weight, offset, 0)
        return (fold_batch(acc, q_blocks, weight, far_ids, onehot), stored)

    acc_start = jnp.zeros((qext.shape[0], nblocks, TILE), jnp.float32)
    stored_start = jnp.zeros((tiles_total, TILE, TILE), jnp.float32)
    acc, stored = lax.fori_loop(0, rounds, hydro_step, (acc_start, stored_start))
    acc = acc.reshape(qext.shape[0], nlocal)
    rate, count_n = hydro_rate(acc, qext[:, :nlocal])
    density_new = density + dt * rate[0]
    momentum_new = momentum + dt * rate[1:4]
    yzero = field + dt * rate[4:7]
    psi_new = (psi + dt * rate[7]) * jnp.exp(-damping * dt * ch)

    def operator(bfl):
        eta = ohmic + fac * jnp.sum(bfl * bfl, axis=0)
        received = spread_ghosts(jnp.concatenate([bfl, eta[None]], axis=0), ghost_index)
        b_ext = extend(bfl, received[0:3])
        eta_ext = extend(eta[None], received[3:4])[0]
        qdiff = jnp.concatenate([b_ext, eta_ext[None] * b_ext, eta_ext[None]], axis=0)
        diff_blocks = qdiff.reshape(7, EXT_BLOCKS, TILE)

        def diff_step(turn, acc_diff):
            offset = (turn * batch).astype(jnp.int32)
            near_ids, far_ids, onehot = batch_lists(offset)
            weight = lax.dynamic_slice_in_dim(stored, offset, batch, 0)
            return fold_batch(acc_diff, diff_blocks, weight, far_ids, onehot)

        acc_diff = lax.fori_loop(0, rounds, diff_step, jnp.zeros((7, nblocks, TILE), jnp.float32))
        return diffusion_rate(acc_diff.reshape(7, nlocal), bfl, eta, count_n)

    first, rows = rkl_table(SECTIONS)
    lzero = operator(yzero)
    older = yzero
    prev = yzero + first * dt * lzero
    for mu_j, nu_j, mut_j, gam_j in rows:
        nxt = (
            mu_j * prev
            + nu_j * older
            + (1.0 - mu_j - nu_j) * yzero
            + mut_j * dt * operator(prev)
            + gam_j * dt * lzero
        )
        older = prev
        prev = nxt
    return (density_new, momentum_new, prev, psi_new)


def solution(mesh):
    placed = (
        P(None, ("gx", "gy")),
        P(("gx", "gy")),
        P(None, ("gx", "gy")),
        P(None, ("gx", "gy")),
        P(("gx", "gy")),
        P(("gx", "gy")),
        P(("gx", "gy")),
        P(("gx", "gy")),
        P(("gx", "gy")),
        P(("gx", "gy")),
        P(("gx", "gy")),
    )
    return jax.shard_map(
        shards,
        mesh=mesh,
        in_specs=placed,
        out_specs=(P(("gx", "gy")), P(None, ("gx", "gy")), P(None, ("gx", "gy")), P(("gx", "gy"))),
        check_vma=False,
    )
```

profile of v0, /device:TPU:55, one launch (start us, length us, event | category | flops | bytes accessed | tf_op | source)
XLA Modules:
  0.0 306.7 jit_solution(18311550818761193361)
XLA Ops:
  0.6 0.9 compare_and_fusion.11
  1.5 0.8 compare_select_fusion.7
  2.4 0.8 compare_and_fusion.12
  3.2 0.8 multiply_reduce_fusion.4
  4.0 1.3 fusion.166
  5.3 0.8 broadcast_divide_fusion
  6.1 1.6 concatenate.175
  9.6 1.1 gather_fusion.8
  11.0 2.3 collective-permute-start
  14.8 1.1 gather_fusion.11
  16.2 3.0 collective-permute-start.1
  20.9 102.0 %pmax.7 = f32[]{:T(128)} all-reduce(f32[]{:T(128)} %get-tuple-element.561), channel_id=1, replica_groups=mesh['gx'=32,'gy'=16] {'gx','gy'}, use_global_device_ids=true, to_apply=%region_2.0 | all-reduce | flops 1 | bytes 8 | tf_op jit(solution)/shard_map/pmax | solution.py:189
  126.7 2.6 collective-permute-start.3
  129.4 3.0 collective-permute-start.2
  132.4 0.8 collective-permute-done.2
  136.5 2.4 broadcast_in_dim.147
  139.0 27.4 %while.57 = (s32[]{:T(128)}, f32[53,16,128]{2,1,0:T(8,128)S(1)}, f32[64,128,128]{2,1,0:T(8,128)}, s32[]{:T(128)}, s32[64]{0:T(128)S(1)}, /*index=5*/f32[3,25,128...) while((s32[]{:T(128)}, f32[53,16,128]{2,1,0:T(8,128)S(1)}, ...), condition=%wide.region_5.10_spmd.clone, body=%wide.region_4.9_spmd.clone.sunk | while | flops 388064800 | bytes 8103835 | solution.py:238
  140.7 3.1 %fusion.228 = f32[64,128,128]{2,1,0:T(8,128)} fusion(f32[64,128,128]{2,1,0:T(8,128)} %get-tuple-element.1045, s32[]{:T(128)S(6)} %select_n.425, f32[32,128]{1,0:T(8,128)S(1)} %bitcast.557, f32[32,128]{1,0:T(8,128)S(1)} %bitcast.563, f32[32,128]{1,0:T(8,128)S(1)} %bitcast.559, f32[32,128]{1,0:T(8,128)S(1)} %bitcast.565, f32[32,128]{1,0:T(8,128)S(1)} %bitcast.555, ...), kind=kLoop, calls=%fused_computation.53.clone.1 | loop fusion | flops 6291456 | bytes 2195460 | tf_op jit(solution)/shard_map/while/body/dynamic_update_slice | solution.py:233
  144.4 7.1 %fusion.226 = f32[53,32,128]{2,0,1:T(8,128)S(1)} fusion(f32[32,128]{1,0:T(8,128)S(1)} %bitcast.558, f32[32,128]{1,0:T(8,128)S(1)} %bitcast.564, f32[32,128]{1,0:T(8,128)S(1)} %bitcast.560, f32[32,128]{1,0:T(8,128)S(1)} %bitcast.566, f32[32,128]{1,0:T(8,128)S(1)} %bitcast.556, f32[32,128]{1,0:T(8,128)S(1)} %bitcast.562, ...), kind=kOutput, calls=%fused_computation.55.clone.1 | convolution fusion | flops 339955712 | bytes 1835040 | tf_op jit(solution)/shard_map/while/body/rtb,tab->rta/dot_general | solution.py:211
  154.4 3.1 %fusion.228 = f32[64,128,128]{2,1,0:T(8,128)} fusion(f32[64,128,128]{2,1,0:T(8,128)} %get-tuple-element.1045, s32[]{:T(128)S(6)} %select_n.425, f32[32,128]{1,0:T(8,128)S(1)} %bitcast.557, f32[32,128]{1,0:T(8,128)S(1)} %bitcast.563, f32[32,128]{1,0:T(8,128)S(1)} %bitcast.559, f32[32,128]{1,0:T(8,128)S(1)} %bitcast.565, f32[32,128]{1,0:T(8,128)S(1)} %bitcast.555, ...), kind=kLoop, calls=%fused_computation.53.clone.1 | loop fusion | flops 6291456 | bytes 2195460 | tf_op jit(solution)/shard_map/while/body/dynamic_update_slice | solution.py:233
  158.1 7.1 %fusion.226 = f32[53,32,128]{2,0,1:T(8,128)S(1)} fusion(f32[32,128]{1,0:T(8,128)S(1)} %bitcast.558, f32[32,128]{1,0:T(8,128)S(1)} %bitcast.564, f32[32,128]{1,0:T(8,128)S(1)} %bitcast.560, f32[32,128]{1,0:T(8,128)S(1)} %bitcast.566, f32[32,128]{1,0:T(8,128)S(1)} %bitcast.556, f32[32,128]{1,0:T(8,128)S(1)} %bitcast.562, ...), kind=kOutput, calls=%fused_computation.55.clone.1 | convolution fusion | flops 339955712 | bytes 1835040 | tf_op jit(solution)/shard_map/while/body/rtb,tab->rta/dot_general | solution.py:211
  168.5 1.1 gather_fusion.16
  170.7 1.1 gather_fusion.19
  174.9 2.6 collective-permute-start.4
  178.1 3.1 %collective-permute-start.5 = (f32[1,4,384]{2,1,0:T(4,128)S(1)}, f32[1,4,384]{2,1,0:T(4,128)S(1)}, u32[]{:S(2)}, u32[]{:S(2)}) collective-permute-start(f32[1,4,384]{2,1,0:T(4,128)S(1)} %maximum_bitcast_fusion.5), channel_id=1, source_target_pairs={{16,0},{32,16},{48,32},{64,48},{80,64},{96,80},{112,96},{128,112},... | collective-permute-start | bytes 18440 | tf_op jit(solution)/shard_map/ppermute | solution.py:29
  182.7 2.8 collective-permute-start.7
  185.5 2.8 collective-permute-start.6
  189.6 13.4 %while.58 = (s32[]{:T(128)}, f32[7,16,128]{2,1,0:T(8,128)S(1)}, s32[]{:T(128)}, f32[64,128,128]{2,1,0:T(8,128)}, s32[64]{0:T(128)S(1)}, /*index=5*/f32[7,25,128]...) while((s32[]{:T(128)}, f32[7,16,128]{2,1,0:T(8,128)S(1)}, ...), condition=%wide.region_8.0_spmd.clone, body=%wide.region_7.16_spmd.clone.sunk | while | flops 49590532 | bytes 2790583 | solution.py:260
  189.8 0.7 compare_and_fusion.20
  191.1 5.0 %fusion.233 = f32[7,32,128]{2,0,1:T(8,128)S(1)} fusion(f32[64,128,128]{2,1,0:T(8,128)} %get-tuple-element.1096, s32[]{:T(128)S(6)} %select_n.427, f32[32,7,128]{2,1,0:T(8,128)S(1)} %gather_fusion.3, pred[32]{0:T(512)(128)(4,1)S(1)} %get-tuple-element.995), kind=kOutput, calls=%fused_computation.92.clone.1 | convolution fusion | flops 44068864 | bytes 2326564 | tf_op jit(solution)/shard_map/while/body/rtb,tab->rta/dot_general | solution.py:211
  196.4 0.7 compare_and_fusion.20
  197.7 5.0 %fusion.233 = f32[7,32,128]{2,0,1:T(8,128)S(1)} fusion(f32[64,128,128]{2,1,0:T(8,128)} %get-tuple-element.1096, s32[]{:T(128)S(6)} %select_n.427, f32[32,7,128]{2,1,0:T(8,128)S(1)} %gather_fusion.3, pred[32]{0:T(512)(128)(4,1)S(1)} %get-tuple-element.995), kind=kOutput, calls=%fused_computation.92.clone.1 | convolution fusion | flops 44068864 | bytes 2326564 | tf_op jit(solution)/shard_map/while/body/rtb,tab->rta/dot_general | solution.py:211
  203.5 1.1 gather_fusion.24
  205.7 1.1 gather_fusion.27
  209.9 2.0 collective-permute-start.8
  212.5 3.3 %collective-permute-start.9 = (f32[1,4,384]{2,1,0:T(4,128)S(1)}, f32[1,4,384]{2,1,0:T(4,128)S(1)}, u32[]{:S(2)}, u32[]{:S(2)}) collective-permute-start(f32[1,4,384]{2,1,0:T(4,128)S(1)} %maximum_bitcast_fusion.7), channel_id=1, source_target_pairs={{16,0},{32,16},{48,32},{64,48},{80,64},{96,80},{112,96},{128,112},... | collective-permute-start | bytes 18440 | tf_op jit(solution)/shard_map/ppermute | solution.py:29
  217.1 2.7 collective-permute-start.11
  219.8 2.9 collective-permute-start.10
  224.0 13.2 %while.59 = (s32[]{:T(128)}, f32[7,16,128]{2,1,0:T(8,128)S(1)}, s32[]{:T(128)}, f32[64,128,128]{2,1,0:T(8,128)}, s32[64]{0:T(128)S(1)}, /*index=5*/f32[7,25,128]...) while((s32[]{:T(128)}, f32[7,16,128]{2,1,0:T(8,128)S(1)}, ...), condition=%wide.region_11.20_spmd.clone, body=%wide.region_10.19_spmd.clone.sunk | while | flops 49590532 | bytes 2790583 | solution.py:260
  224.0 0.7 compare_and_fusion.21
  225.3 5.0 %fusion.239 = f32[7,32,128]{2,0,1:T(8,128)S(1)} fusion(f32[64,128,128]{2,1,0:T(8,128)} %get-tuple-element.1132, s32[]{:T(128)S(6)} %select_n.429, f32[32,7,128]{2,1,0:T(8,128)S(1)} %gather_fusion.4, pred[32]{0:T(512)(128)(4,1)S(1)} %get-tuple-element.1006), kind=kOutput, calls=%fused_computation.113.clone.1 | convolution fusion | flops 44068864 | bytes 2326564 | tf_op jit(solution)/shard_map/while/body/rtb,tab->rta/dot_general | solution.py:211
  230.6 0.7 compare_and_fusion.21
  231.9 5.0 %fusion.239 = f32[7,32,128]{2,0,1:T(8,128)S(1)} fusion(f32[64,128,128]{2,1,0:T(8,128)} %get-tuple-element.1132, s32[]{:T(128)S(6)} %select_n.429, f32[32,7,128]{2,1,0:T(8,128)S(1)} %gather_fusion.4, pred[32]{0:T(512)(128)(4,1)S(1)} %get-tuple-element.1006), kind=kOutput, calls=%fused_computation.113.clone.1 | convolution fusion | flops 44068864 | bytes 2326564 | tf_op jit(solution)/shard_map/while/body/rtb,tab->rta/dot_general | solution.py:211
  237.7 1.1 gather_fusion.32
  239.9 1.1 gather_fusion.35
  244.1 1.9 collective-permute-start.12
  246.7 3.4 %collective-permute-start.13 = (f32[1,4,384]{2,1,0:T(4,128)S(1)}, f32[1,4,384]{2,1,0:T(4,128)S(1)}, u32[]{:S(2)}, u32[]{:S(2)}) collective-permute-start(f32[1,4,384]{2,1,0:T(4,128)S(1)} %maximum_bitcast_fusion.9), channel_id=1, source_target_pairs={{16,0},{32,16},{48,32},{64,48},{80,64},{96,80},{112,96},{128,112},... | collective-permute-start | bytes 18440 | tf_op jit(solution)/shard_map/ppermute | solution.py:29
  251.2 2.7 collective-permute-start.15
  253.9 2.9 collective-permute-start.14
  258.1 13.4 %while.60 = (s32[]{:T(128)}, f32[7,16,128]{2,1,0:T(8,128)S(1)}, s32[]{:T(128)}, f32[64,128,128]{2,1,0:T(8,128)}, s32[64]{0:T(128)S(1)}, /*index=5*/f32[7,25,128]...) while((s32[]{:T(128)}, f32[7,16,128]{2,1,0:T(8,128)S(1)}, ...), condition=%wide.region_14.23_spmd.clone, body=%wide.region_13.22_spmd.clone.sunk | while | flops 49590532 | bytes 2790583 | solution.py:260
  258.3 0.7 compare_and_fusion.22
  259.7 5.0 %fusion.245 = f32[7,32,128]{2,0,1:T(8,128)S(1)} fusion(f32[64,128,128]{2,1,0:T(8,128)} %get-tuple-element.1168, s32[]{:T(128)S(6)} %select_n.431, f32[32,7,128]{2,1,0:T(8,128)S(1)} %gather_fusion.5, pred[32]{0:T(512)(128)(4,1)S(1)} %get-tuple-element.1017), kind=kOutput, calls=%fused_computation.134.clone.1 | convolution fusion | flops 44068864 | bytes 2326564 | tf_op jit(solution)/shard_map/while/body/rtb,tab->rta/dot_general | solution.py:211
  264.9 0.7 compare_and_fusion.22
  266.3 5.0 %fusion.245 = f32[7,32,128]{2,0,1:T(8,128)S(1)} fusion(f32[64,128,128]{2,1,0:T(8,128)} %get-tuple-element.1168, s32[]{:T(128)S(6)} %select_n.431, f32[32,7,128]{2,1,0:T(8,128)S(1)} %gather_fusion.5, pred[32]{0:T(512)(128)(4,1)S(1)} %get-tuple-element.1017), kind=kOutput, calls=%fused_computation.134.clone.1 | convolution fusion | flops 44068864 | bytes 2326564 | tf_op jit(solution)/shard_map/while/body/rtb,tab->rta/dot_general | solution.py:211
  274.5 1.1 gather_fusion.40
  275.6 1.1 gather_fusion.43
  278.5 1.9 collective-permute-start.16
  281.0 3.4 %collective-permute-start.17 = (f32[1,4,384]{2,1,0:T(4,128)S(1)}, f32[1,4,384]{2,1,0:T(4,128)S(1)}, u32[]{:S(2)}, u32[]{:S(2)}) collective-permute-start(f32[1,4,384]{2,1,0:T(4,128)S(1)} %maximum_bitcast_fusion.11), channel_id=1, source_target_pairs={{16,0},{32,16},{48,32},{64,48},{80,64},{96,80},{112,96},{128,112},... | collective-permute-start | bytes 18440 | tf_op jit(solution)/shard_map/ppermute | solution.py:29
  284.5 1.2 collective-permute-done.17
  285.8 2.4 collective-permute-start.19
  288.3 3.2 %collective-permute-start.18 = (f32[1,4,224]{2,1,0:T(4,128)S(1)}, f32[1,4,224]{2,1,0:T(4,128)S(1)}, u32[]{:S(2)}, u32[]{:S(2)}) collective-permute-start(f32[1,4,224]{2,1,0:T(4,128)S(1)} %maximum_bitcast_fusion.18), channel_id=1, source_target_pairs={{0,1},{1,2},{2,3},{3,4},{4,5},{5,6},{6,7},{7,8},{8,9},{9,10},{10,1... | collective-permute-start | bytes 10760 | tf_op jit(solution)/shard_map/ppermute | solution.py:28
  292.7 13.2 %while.61 = (s32[]{:T(128)}, f32[7,16,128]{2,1,0:T(8,128)S(1)}, s32[]{:T(128)}, f32[64,128,128]{2,1,0:T(8,128)}, s32[64]{0:T(128)S(1)}, /*index=5*/f32[7,25,128]...) while((s32[]{:T(128)}, f32[7,16,128]{2,1,0:T(8,128)S(1)}, ...), condition=%wide.region_17.26_spmd.clone, body=%wide.region_16.25_spmd.clone.sunk | while | flops 49590532 | bytes 2790583 | solution.py:260
  294.1 5.0 %fusion.251 = f32[7,32,128]{2,0,1:T(8,128)S(1)} fusion(f32[64,128,128]{2,1,0:T(8,128)} %get-tuple-element.1204, s32[]{:T(128)S(6)} %select_n.433, f32[32,7,128]{2,1,0:T(8,128)S(1)} %gather_fusion.6, pred[32]{0:T(512)(128)(4,1)S(1)} %get-tuple-element.1028), kind=kOutput, calls=%fused_computation.155.clone.1 | convolution fusion | flops 44068864 | bytes 2326564 | tf_op jit(solution)/shard_map/while/body/rtb,tab->rta/dot_general | solution.py:211
  300.7 5.0 %fusion.251 = f32[7,32,128]{2,0,1:T(8,128)S(1)} fusion(f32[64,128,128]{2,1,0:T(8,128)} %get-tuple-element.1204, s32[]{:T(128)S(6)} %select_n.433, f32[32,7,128]{2,1,0:T(8,128)S(1)} %gather_fusion.6, pred[32]{0:T(512)(128)(4,1)S(1)} %get-tuple-element.1028), kind=kOutput, calls=%fused_computation.155.clone.1 | convolution fusion | flops 44068864 | bytes 2326564 | tf_op jit(solution)/shard_map/while/body/rtb,tab->rta/dot_general | solution.py:211
  (376 shorter events, 56.9 us)
Async XLA Ops:
  0.6 18.5 %copy-start.7 = (s32[1088]{0:T(1024)S(1)}, s32[1088]{0:T(1024)}, u32[]{:S(2)}) copy-start(s32[1088]{0:T(1024)} %param.44) | copy-start | bytes 13060
  11.0 115.5 %collective-permute-start = (f32[1,13,384]{2,1,0:T(8,128)S(1)}, f32[1,13,384]{2,1,0:T(8,128)S(1)}, u32[]{:S(2)}, u32[]{:S(2)}) collective-permute-start(f32[1,13,384]{2,1,0:T(8,128)S(1)} %maximum_bitcast_fusion), channel_id=1, source_target_pairs={{0,16},{16,32},{32,48},{48,64},{64,80},{80,96},{96,112},{112,128},... | collective-permute-start | bytes 59912 | tf_op jit(solution)/shard_map/ppermute | solution.py:28
  16.2 110.4 %collective-permute-start.1 = (f32[1,13,384]{2,1,0:T(8,128)S(1)}, f32[1,13,384]{2,1,0:T(8,128)S(1)}, u32[]{:S(2)}, u32[]{:S(2)}) collective-permute-start(f32[1,13,384]{2,1,0:T(8,128)S(1)} %maximum_bitcast_fusion.1), channel_id=1, source_target_pairs={{16,0},{32,16},{48,32},{64,48},{80,64},{96,80},{112,96},{128,112},... | collective-permute-start | bytes 59912 | tf_op jit(solution)/shard_map/ppermute | solution.py:29
  126.7 5.6 %collective-permute-start.3 = (f32[1,13,224]{2,1,0:T(8,128)S(1)}, f32[1,13,224]{2,1,0:T(8,128)S(1)}, u32[]{:S(2)}, u32[]{:S(2)}) collective-permute-start(f32[1,13,224]{2,1,0:T(8,128)S(1)} %maximum_bitcast_fusion.3), channel_id=1, source_target_pairs={{1,0},{2,1},{3,2},{4,3},{5,4},{6,5},{7,6},{8,7},{9,8},{10,9},{11,1... | collective-permute-start | bytes 34952 | tf_op jit(solution)/shard_map/ppermute | solution.py:29
  129.4 3.8 %collective-permute-start.2 = (f32[1,13,224]{2,1,0:T(8,128)S(1)}, f32[1,13,224]{2,1,0:T(8,128)S(1)}, u32[]{:S(2)}, u32[]{:S(2)}) collective-permute-start(f32[1,13,224]{2,1,0:T(8,128)S(1)} %maximum_bitcast_fusion.2), channel_id=1, source_target_pairs={{0,1},{1,2},{2,3},{3,4},{4,5},{5,6},{6,7},{7,8},{8,9},{9,10},{10,1... | collective-permute-start | bytes 34952 | tf_op jit(solution)/shard_map/ppermute | solution.py:28
  136.4 2.5 copy-start
  136.5 2.5 copy-start.8
  139.0 27.6 %copy-start.5 = (f32[3,2048]{1,0:T(4,128)S(1)}, f32[3,2048]{1,0:T(4,128)}, u32[]{:S(2)}) copy-start(f32[3,2048]{1,0:T(4,128)} %param.37) | copy-start | bytes 73732
  139.0 27.8 %copy-start.1 = (f32[3,2048]{1,0:T(4,128)S(1)}, f32[3,2048]{1,0:T(4,128)}, u32[]{:S(2)}) copy-start(f32[3,2048]{1,0:T(4,128)} %param.40) | copy-start | bytes 73732
  139.0 27.8 %copy-start.2 = (f32[3,2048]{1,0:T(4,128)S(1)}, f32[3,2048]{1,0:T(4,128)}, u32[]{:S(2)}) copy-start(f32[3,2048]{1,0:T(4,128)} %param.39) | copy-start | bytes 73732
  166.4 1.1 copy-start.3
  166.4 1.1 copy-start.4
  166.4 1.0 copy-start.9
  166.6 14.9 %copy-start.6 = (f32[2048]{0:T(1024)S(1)}, f32[2048]{0:T(1024)}, u32[]{:S(2)}) copy-start(f32[2048]{0:T(1024)} %param.41) | copy-start | bytes 24580
  174.9 7.3 %collective-permute-start.4 = (f32[1,4,384]{2,1,0:T(4,128)S(1)}, f32[1,4,384]{2,1,0:T(4,128)S(1)}, u32[]{:S(2)}, u32[]{:S(2)}) collective-permute-start(f32[1,4,384]{2,1,0:T(4,128)S(1)} %maximum_bitcast_fusion.4), channel_id=1, source_target_pairs={{0,16},{16,32},{32,48},{48,64},{64,80},{80,96},{96,112},{112,128},... | collective-permute-start | bytes 18440 | tf_op jit(solution)/shard_map/ppermute | solution.py:28
  178.1 4.4 %collective-permute-start.5 = (f32[1,4,384]{2,1,0:T(4,128)S(1)}, f32[1,4,384]{2,1,0:T(4,128)S(1)}, u32[]{:S(2)}, u32[]{:S(2)}) collective-permute-start(f32[1,4,384]{2,1,0:T(4,128)S(1)} %maximum_bitcast_fusion.5), channel_id=1, source_target_pairs={{16,0},{32,16},{48,32},{64,48},{80,64},{96,80},{112,96},{128,112},... | collective-permute-start | bytes 18440 | tf_op jit(solution)/shard_map/ppermute | solution.py:29
  182.7 5.6 %collective-permute-start.7 = (f32[1,4,224]{2,1,0:T(4,128)S(1)}, f32[1,4,224]{2,1,0:T(4,128)S(1)}, u32[]{:S(2)}, u32[]{:S(2)}) collective-permute-start(f32[1,4,224]{2,1,0:T(4,128)S(1)} %maximum_bitcast_fusion.13), channel_id=1, source_target_pairs={{1,0},{2,1},{3,2},{4,3},{5,4},{6,5},{7,6},{8,7},{9,8},{10,9},{11,1... | collective-permute-start | bytes 10760 | tf_op jit(solution)/shard_map/ppermute | solution.py:29
  185.5 3.5 %collective-permute-start.6 = (f32[1,4,224]{2,1,0:T(4,128)S(1)}, f32[1,4,224]{2,1,0:T(4,128)S(1)}, u32[]{:S(2)}, u32[]{:S(2)}) collective-permute-start(f32[1,4,224]{2,1,0:T(4,128)S(1)} %maximum_bitcast_fusion.12), channel_id=1, source_target_pairs={{0,1},{1,2},{2,3},{3,4},{4,5},{5,6},{6,7},{7,8},{8,9},{9,10},{10,1... | collective-permute-start | bytes 10760 | tf_op jit(solution)/shard_map/ppermute | solution.py:28
  209.9 6.3 %collective-permute-start.8 = (f32[1,4,384]{2,1,0:T(4,128)S(1)}, f32[1,4,384]{2,1,0:T(4,128)S(1)}, u32[]{:S(2)}, u32[]{:S(2)}) collective-permute-start(f32[1,4,384]{2,1,0:T(4,128)S(1)} %maximum_bitcast_fusion.6), channel_id=1, source_target_pairs={{0,16},{16,32},{32,48},{48,64},{64,80},{80,96},{96,112},{112,128},... | collective-permute-start | bytes 18440 | tf_op jit(solution)/shard_map/ppermute | solution.py:28
  212.5 4.4 %collective-permute-start.9 = (f32[1,4,384]{2,1,0:T(4,128)S(1)}, f32[1,4,384]{2,1,0:T(4,128)S(1)}, u32[]{:S(2)}, u32[]{:S(2)}) collective-permute-start(f32[1,4,384]{2,1,0:T(4,128)S(1)} %maximum_bitcast_fusion.7), channel_id=1, source_target_pairs={{16,0},{32,16},{48,32},{64,48},{80,64},{96,80},{112,96},{128,112},... | collective-permute-start | bytes 18440 | tf_op jit(solution)/shard_map/ppermute | solution.py:29
  217.1 5.6 %collective-permute-start.11 = (f32[1,4,224]{2,1,0:T(4,128)S(1)}, f32[1,4,224]{2,1,0:T(4,128)S(1)}, u32[]{:S(2)}, u32[]{:S(2)}) collective-permute-start(f32[1,4,224]{2,1,0:T(4,128)S(1)} %maximum_bitcast_fusion.15), channel_id=1, source_target_pairs={{1,0},{2,1},{3,2},{4,3},{5,4},{6,5},{7,6},{8,7},{9,8},{10,9},{11,1... | collective-permute-start | bytes 10760 | tf_op jit(solution)/shard_map/ppermute | solution.py:29
  219.8 3.6 %collective-permute-start.10 = (f32[1,4,224]{2,1,0:T(4,128)S(1)}, f32[1,4,224]{2,1,0:T(4,128)S(1)}, u32[]{:S(2)}, u32[]{:S(2)}) collective-permute-start(f32[1,4,224]{2,1,0:T(4,128)S(1)} %maximum_bitcast_fusion.14), channel_id=1, source_target_pairs={{0,1},{1,2},{2,3},{3,4},{4,5},{5,6},{6,7},{7,8},{8,9},{9,10},{10,1... | collective-permute-start | bytes 10760 | tf_op jit(solution)/shard_map/ppermute | solution.py:28
  244.1 6.3 %collective-permute-start.12 = (f32[1,4,384]{2,1,0:T(4,128)S(1)}, f32[1,4,384]{2,1,0:T(4,128)S(1)}, u32[]{:S(2)}, u32[]{:S(2)}) collective-permute-start(f32[1,4,384]{2,1,0:T(4,128)S(1)} %maximum_bitcast_fusion.8), channel_id=1, source_target_pairs={{0,16},{16,32},{32,48},{48,64},{64,80},{80,96},{96,112},{112,128},... | collective-permute-start | bytes 18440 | tf_op jit(solution)/shard_map/ppermute | solution.py:28
  246.7 4.4 %collective-permute-start.13 = (f32[1,4,384]{2,1,0:T(4,128)S(1)}, f32[1,4,384]{2,1,0:T(4,128)S(1)}, u32[]{:S(2)}, u32[]{:S(2)}) collective-permute-start(f32[1,4,384]{2,1,0:T(4,128)S(1)} %maximum_bitcast_fusion.9), channel_id=1, source_target_pairs={{16,0},{32,16},{48,32},{64,48},{80,64},{96,80},{112,96},{128,112},... | collective-permute-start | bytes 18440 | tf_op jit(solution)/shard_map/ppermute | solution.py:29
  251.2 5.6 %collective-permute-start.15 = (f32[1,4,224]{2,1,0:T(4,128)S(1)}, f32[1,4,224]{2,1,0:T(4,128)S(1)}, u32[]{:S(2)}, u32[]{:S(2)}) collective-permute-start(f32[1,4,224]{2,1,0:T(4,128)S(1)} %maximum_bitcast_fusion.17), channel_id=1, source_target_pairs={{1,0},{2,1},{3,2},{4,3},{5,4},{6,5},{7,6},{8,7},{9,8},{10,9},{11,1... | collective-permute-start | bytes 10760 | tf_op jit(solution)/shard_map/ppermute | solution.py:29
  253.9 3.6 %collective-permute-start.14 = (f32[1,4,224]{2,1,0:T(4,128)S(1)}, f32[1,4,224]{2,1,0:T(4,128)S(1)}, u32[]{:S(2)}, u32[]{:S(2)}) collective-permute-start(f32[1,4,224]{2,1,0:T(4,128)S(1)} %maximum_bitcast_fusion.16), channel_id=1, source_target_pairs={{0,1},{1,2},{2,3},{3,4},{4,5},{5,6},{6,7},{7,8},{8,9},{9,10},{10,1... | collective-permute-start | bytes 10760 | tf_op jit(solution)/shard_map/ppermute | solution.py:28
  278.5 6.0 %collective-permute-start.16 = (f32[1,4,384]{2,1,0:T(4,128)S(1)}, f32[1,4,384]{2,1,0:T(4,128)S(1)}, u32[]{:S(2)}, u32[]{:S(2)}) collective-permute-start(f32[1,4,384]{2,1,0:T(4,128)S(1)} %maximum_bitcast_fusion.10), channel_id=1, source_target_pairs={{0,16},{16,32},{32,48},{48,64},{64,80},{80,96},{96,112},{112,128},... | collective-permute-start | bytes 18440 | tf_op jit(solution)/shard_map/ppermute | solution.py:28
  281.0 4.7 %collective-permute-start.17 = (f32[1,4,384]{2,1,0:T(4,128)S(1)}, f32[1,4,384]{2,1,0:T(4,128)S(1)}, u32[]{:S(2)}, u32[]{:S(2)}) collective-permute-start(f32[1,4,384]{2,1,0:T(4,128)S(1)} %maximum_bitcast_fusion.11), channel_id=1, source_target_pairs={{16,0},{32,16},{48,32},{64,48},{80,64},{96,80},{112,96},{128,112},... | collective-permute-start | bytes 18440 | tf_op jit(solution)/shard_map/ppermute | solution.py:29
  285.8 5.6 %collective-permute-start.19 = (f32[1,4,224]{2,1,0:T(4,128)S(1)}, f32[1,4,224]{2,1,0:T(4,128)S(1)}, u32[]{:S(2)}, u32[]{:S(2)}) collective-permute-start(f32[1,4,224]{2,1,0:T(4,128)S(1)} %maximum_bitcast_fusion.19), channel_id=1, source_target_pairs={{1,0},{2,1},{3,2},{4,3},{5,4},{6,5},{7,6},{8,7},{9,8},{10,9},{11,1... | collective-permute-start | bytes 10760 | tf_op jit(solution)/shard_map/ppermute | solution.py:29
  288.3 3.9 %collective-permute-start.18 = (f32[1,4,224]{2,1,0:T(4,128)S(1)}, f32[1,4,224]{2,1,0:T(4,128)S(1)}, u32[]{:S(2)}, u32[]{:S(2)}) collective-permute-start(f32[1,4,224]{2,1,0:T(4,128)S(1)} %maximum_bitcast_fusion.18), channel_id=1, source_target_pairs={{0,1},{1,2},{2,3},{3,4},{4,5},{5,6},{6,7},{7,8},{8,9},{9,10},{10,1... | collective-permute-start | bytes 10760 | tf_op jit(solution)/shard_map/ppermute | solution.py:28
where the time goes:
time: 308 us; the launch traced here: 307 us
  blocking collectives  102 us (33%)
  matrix products  56.6 us (18%)
  starting transfers between devices  54.6 us (18%)
  local copies, waits for them, and re-layouts  51.5 us (17%)
  other arithmetic  29.5 us (10%)
  waiting for transfers between devices  5.96 us (2%)
  between operations  5.47 us (2%)
    pmax x1, blocking collectives, shards(): ch = lax.pmax(jnp.max(speed), ('gx', 'gy'))  102 us
    dot_general x10, matrix products, fold_batch(): jnp.einsum('rtb,tab->rta', qsel, weight, precision=lax.Precision.HIGHEST,...  53.9 us
    ppermute x10, starting transfers between devices, extended(): after = lax.ppermute(leading, axis, down)  29.1 us
    gather x40, local copies, waits for them, and re-layouts, spread_ghosts(): jnp.take(rows, ghost_index[starts[d]:starts[d] + sizes[d]], axis=1)  29.1 us
    ppermute x10, starting transfers between devices, extended(): before = lax.ppermute(last, axis, up)  25.4 us
    dynamic_update_slice x2, other arithmetic, hydro_step(): stored = lax.dynamic_update_slice_in_dim(stored, weight, offset, 0)  6.18 us
  transfers between devices with their start and end apart: 20, of which 9 were waited for; matrix products, arithmetic and copies ran while one was open for 3% of the time, Pallas kernels for 0%

commit v1 on v0

v1 whole, which is shorter than its diff:
```python
import jax
import jax.numpy as jnp
from jax import lax
from jax.experimental import pallas as pl
from jax.experimental.pallas import tpu as pltpu
from jax.sharding import PartitionSpec as P

TILE = 128
SECTIONS = 4
SIZES = [32, 320, 32, 160, 160, 32, 320, 32]
DIRECTIONS = [(-1, -1), (-1, 0), (-1, 1), (0, -1), (0, 1), (1, -1), (1, 0), (1, 1)]
STARTS = [sum(SIZES[:d]) for d in range(8)]
BLOCKS = 16
GBLOCKS = 9
TILES = 64
COURANT = 0.3
DAMPING = 0.5
MESH = pl.DeviceIdType.MESH
F32 = jnp.float32
BF16 = jnp.bfloat16

PIECES = []
OFFSET = []
for d in range(8):
    OFFSET.append(len(PIECES))
    for k in range(STARTS[d] // TILE, (STARTS[d] + SIZES[d] - 1) // TILE + 1):
        lo = max(STARTS[d] - k * TILE, 0)
        hi = min(STARTS[d] + SIZES[d] - k * TILE, TILE)
        PIECES.append((d, k, lo, hi))
COUNT = [sum(1 for p in PIECES if p[0] == d) for d in range(8)]
NPIECE = len(PIECES)

QROWS = 40


def rkl_table(sections):
    wfirst = 4.0 / (sections * sections + sections - 2)
    bvals = [1.0 / 3.0] * 3 + [(j * j + j - 2) / (2.0 * j * (j + 1)) for j in range(3, sections + 1)]
    rows = [(1.0, 0.0, 0.0, bvals[1] * wfirst, 0.0)]
    for j in range(2, sections + 1):
        mu = (2.0 * j - 1.0) / j * bvals[j] / bvals[j - 1]
        nu = -(j - 1.0) / j * bvals[j] / bvals[j - 2]
        mut = mu * wfirst
        rows.append((mu, nu, 1.0 - mu - nu, mut, -(1.0 - bvals[j - 1]) * mut))
    return rows


def q_rows(x, live, rho, mom, bfl, psi, speed):
    inv = 1.0 / rho
    vel = [m * inv for m in mom]
    ptot = rho + 0.5 * (bfl[0] * bfl[0] + bfl[1] * bfl[1] + bfl[2] * bfl[2])
    state = [rho, *mom, *bfl, psi]
    t = {}
    for a in range(3):
        for b in range(a, 3):
            v = mom[b] * vel[a] - bfl[b] * bfl[a]
            t[a, b] = t[b, a] = v + ptot if a == b else v
    ind = {}
    for a in range(3):
        for b in range(a + 1, 3):
            ind[a, b] = vel[a] * bfl[b] - bfl[a] * vel[b]
    gsum = [x[0] * mom[0] + x[1] * mom[1] + x[2] * mom[2]]
    for k in range(3):
        gsum.append(x[0] * t[0, k] + x[1] * t[1, k] + x[2] * t[2, k])
    gsum.append(x[0] * psi - x[1] * ind[0, 1] - x[2] * ind[0, 2])
    gsum.append(x[0] * ind[0, 1] + x[1] * psi - x[2] * ind[1, 2])
    gsum.append(x[0] * ind[0, 2] + x[1] * ind[1, 2] + x[2] * psi)
    gsum.append(x[0] * bfl[0] + x[1] * bfl[1] + x[2] * bfl[2])
    return [
        live, *x, *state, *[speed * u for u in state], speed,
        t[0, 0], t[0, 1], t[0, 2], t[1, 1], t[1, 2], t[2, 2],
        ind[0, 1], ind[0, 2], ind[1, 2], *gsum,
    ]


def flux_of(q):
    m, b, psi = q[5:8], q[8:11], q[11]
    t = {(0, 0): q[21], (0, 1): q[22], (0, 2): q[23], (1, 1): q[24], (1, 2): q[25], (2, 2): q[26]}
    i01, i02, i12 = q[27:30]
    ind = [[psi, i01, i02], [-i01, psi, i12], [-i02, -i12, psi]]
    return [[m[d], *[t[min(d, k), max(d, k)] for k in range(3)], *ind[d], b[d]] for d in range(3)]


def kernel(
    tab, pos, rho_r, mom_r, bfl_r, psi_r, ohm_r, amb_r, gi_r,
    rho_o, mom_o, bfl_o, psi_o,
    pk, lane_b, blk_b, pay, paysend, payrecv, ghp, qp, qt, qb, xn, xt, wst, acch, acct,
    qdl, dsend, drecv, qdb, accd, acdt, yz, prev, older, lz, nloc, etas, facs,
    mxs, mxa, mxb, mxc,
    s_pay, r_pay, s_d, r_d, s_a, r_a, s_b, r_b, s_c, r_c,
):
    ix, iy = lax.axis_index("gx"), lax.axis_index("gy")
    xx, xy = ix // 8, ix % 8

    def near(p, q):
        return ((ix + 32 + p) % 32, (iy + 16 + q) % 16)

    def dev_a(k):
        return (ix, (iy + k) % 16)

    def dev_b(k):
        return (xx * 8 + (xy + k) % 8, iy)

    def dev_c(k):
        return (((xx + k) % 4) * 8 + xy, iy)

    barrier = pltpu.get_barrier_semaphore()

    def hello(dev, n):
        def body(k, c):
            pl.semaphore_signal(barrier, inc=1, device_id=dev(k), device_id_type=MESH)
            return c

        lax.fori_loop(1, n, body, 0)

    hello(dev_a, 16)
    hello(dev_b, 8)
    hello(dev_c, 4)
    for p, q in DIRECTIONS:
        if p:
            pl.semaphore_signal(barrier, inc=1, device_id=near(p, q), device_id_type=MESH)

    for j in range(BLOCKS):
        for n, ref in enumerate((pos, mom_r, bfl_r)):
            pk[pl.ds(48 * n + j, 3, stride=16), :] = ref[:, TILE * j : TILE * (j + 1)]

    def packed(n):
        return pk[16 * n : 16 * (n + 1), :]

    ixf = ix.astype(F32)
    iyf = iy.astype(F32)
    rho = rho_r[...]
    x = [packed(0), packed(1), packed(2)]
    mom = [packed(3), packed(4), packed(5)]
    bfl = [packed(6), packed(7), packed(8)]
    psi = psi_r[...]
    speed = jnp.sqrt(1.0 + (bfl[0] * bfl[0] + bfl[1] * bfl[1] + bfl[2] * bfl[2]) / rho)
    facs[...] = amb_r[...] / (rho * jnp.sqrt(rho))
    mxs[0] = jnp.max(speed, axis=0, keepdims=True)
    live = jnp.ones_like(rho)
    zero = jnp.zeros_like(rho)
    for r, v in enumerate([*x, live, rho, *mom, *bfl, psi, speed, zero, zero, zero]):
        pay[pl.ds(r, 16, stride=16), :] = v

    pl.semaphore_wait(barrier, 15 + 7 + 3 + 6)

    def ring(dev, n, src, dst, ss, rs):
        def one(k):
            return pltpu.make_async_remote_copy(
                src_ref=mxs.at[src], dst_ref=dst.at[k], send_sem=ss.at[k], recv_sem=rs.at[k],
                device_id=dev(k), device_id_type=MESH,
            )

        def send():
            lax.fori_loop(1, n, lambda k, c: (one(k).start(), c)[1], 0)

        def wait():
            def body(k, c):
                one(k).wait_send()
                one(k).wait_recv()
                return c

            lax.fori_loop(1, n, body, 0)
            return lax.fori_loop(1, n, lambda k, c: jnp.maximum(c, dst[k]), mxs[src])

        return send, wait

    send_a, wait_a = ring(dev_a, 16, 0, mxa, s_a, r_a)
    send_b, wait_b = ring(dev_b, 8, 1, mxb, s_b, r_b)
    send_c, wait_c = ring(dev_c, 4, 2, mxc, s_c, r_c)
    send_a()

    gi = gi_r[...]
    for o in range(GBLOCKS):
        row = jnp.broadcast_to(gi[o : o + 1, :], (8, TILE))
        lane_b[o] = row & 127
        blk_b[o] = row >> 7

    lanes = lax.broadcasted_iota(jnp.int32, (8, TILE), 1)

    def gathered(load):
        def body(s, got):
            src = load(s)
            new = []
            for o in range(GBLOCKS):
                val = jnp.take_along_axis(src, lane_b[o], axis=1, mode="promise_in_bounds")
                new.append(jnp.where(blk_b[o] == s, val, got[o]))
            return tuple(new)

        return lax.fori_loop(0, BLOCKS, body, tuple(jnp.zeros((8, TILE), F32) for _ in range(GBLOCKS)))

    def shifted(got):
        out = []
        for d, k, lo, hi in PIECES:
            shift = STARTS[d] - STARTS[7 - d]
            a, s = shift // TILE, shift % TILE
            if lo >= s:
                out.append(pltpu.roll(got[k - a], s, 1) if s else got[k - a])
            elif hi <= s:
                out.append(pltpu.roll(got[k - a - 1], s, 1))
            else:
                out.append(
                    jnp.where(lanes >= s, pltpu.roll(got[k - a], s, 1), pltpu.roll(got[k - a - 1], s, 1))
                )
        return out

    exists = []
    for p, q in DIRECTIONS:
        e = (ix + p >= 0) & (ix + p < 32) & (iy + q >= 0) & (iy + q < 16)
        exists.append(e)

    def combined(load):
        out = []
        for k in range(GBLOCKS):
            tile = jnp.zeros((8, TILE), F32)
            for n, (d, kk, lo, hi) in enumerate(PIECES):
                if kk == k:
                    mask = (lanes >= lo) & (lanes < hi) & exists[d]
                    tile = jnp.where(mask, load(n), tile)
            out.append(tile)
        return out

    def copies(src, dst, ss, rs):
        out = []
        for d, (p, q) in enumerate(DIRECTIONS):
            part = pl.ds(OFFSET[d], COUNT[d])
            out.append(
                pltpu.make_async_remote_copy(
                    src_ref=src.at[part], dst_ref=dst.at[part], send_sem=ss.at[d], recv_sem=rs.at[d],
                    device_id=near(-p, -q), device_id_type=MESH,
                )
            )
        return out

    for g in range(2):
        got = gathered(lambda s, g=g: pay[pl.ds(pl.multiple_of(16 * s + 8 * g, 8), 8), :])
        for n, v in enumerate(shifted(got)):
            paysend[n, 8 * g : 8 * (g + 1), :] = v
    pay_copies = copies(paysend, payrecv, s_pay, r_pay)
    for c in pay_copies:
        c.start()

    def put_q(rows, base):
        for r, v in enumerate(rows):
            qt[pl.ds(base * QROWS + r, 16, stride=QROWS), :] = v

    qloc = q_rows([x[0] - ixf, x[1] - iyf, x[2]], live, rho, mom, bfl, psi, speed)
    for r, v in enumerate(qloc):
        qp[r] = v
    put_q([*qloc, zero, zero], 0)

    mxs[1] = wait_a()
    send_b()

    def put_x(j):
        tile = qt[pl.ds(pl.multiple_of(j * QROWS, 8), 8), :]
        xn[j] = tile
        xt[j] = jnp.transpose(tile)

    def split(j):
        v = qt[pl.ds(pl.multiple_of(j * QROWS, 8), QROWS), :]
        hi = v.astype(BF16).astype(F32)
        qb[j] = jnp.concatenate([hi, v - hi], axis=0).astype(BF16)

    def prep(j, c):
        put_x(j)
        split(j)
        return c

    lax.fori_loop(0, BLOCKS, prep, 0)
    mxs[2] = wait_b()
    send_c()

    for c in pay_copies:
        c.wait_recv()
    for g in range(2):
        tiles = combined(lambda n, g=g: payrecv[n, 8 * g : 8 * (g + 1), :])
        for k, v in enumerate(tiles):
            ghp[16 * k + 8 * g : 16 * k + 8 * g + 8, :] = v
    gh = [ghp[pl.ds(r, 16, stride=16), :] for r in range(13)]
    glive = gh[3]
    grho = jnp.where(glive > 0.0, gh[4], 1.0)
    gq = q_rows(
        [glive * (gh[0] - ixf), glive * (gh[1] - iyf), gh[2]], glive, grho, gh[5:8], gh[8:11], gh[11], gh[12]
    )
    gq = [jnp.where(glive > 0.0, v, 0.0) for v in gq]
    put_q([*gq, zero, zero], BLOCKS)
    lax.fori_loop(BLOCKS, BLOCKS + GBLOCKS, prep, 0)

    def fold(run, part, same):
        return part + jnp.where(same == 1, run, 0.0)

    def hydro_tile(t, run):
        i, j = tab[t], tab[64 + t]
        a, b = xn[i], xt[j]
        d0 = a[1:2, :] - b[:, 1:2]
        d1 = a[2:3, :] - b[:, 2:3]
        d2 = a[3:4, :] - b[:, 3:4]
        base = jnp.maximum(1.0 - 4.0 * (d0 * d0 + d1 * d1 + d2 * d2), 0.0)
        w = base * base
        hi = w.astype(BF16)
        lo = (w - hi.astype(F32)).astype(BF16)
        w2 = jnp.concatenate([hi, lo], axis=0)
        wst[t] = w2
        q = qb[j]
        part = jnp.dot(jnp.concatenate([q, q], axis=1), w2, preferred_element_type=F32)
        run = fold(run, part[:QROWS] + part[QROWS:], tab[128 + t])
        acch[t] = run
        return run

    def unrolled(body, n, start, by):
        def step(s, c):
            for u in range(by):
                c = body(s * by + u, c)
            return c

        return lax.fori_loop(0, n // by, step, start)

    acch[TILES] = jnp.zeros((QROWS, TILE), F32)
    accd[TILES] = jnp.zeros((8, TILE), F32)
    unrolled(hydro_tile, TILES, jnp.zeros((QROWS, TILE), F32), 4)
    for i in range(BLOCKS):
        acct[QROWS * i : QROWS * (i + 1), :] = acch[tab[192 + i]]

    chm = jnp.max(wait_c(), axis=1, keepdims=True)
    ch = jnp.broadcast_to(chm, (BLOCKS, TILE))
    dt = COURANT / ch

    acc = [acct[pl.ds(r, 16, stride=QROWS), :] for r in range(38)]
    qloc = [qp[r] for r in range(38)]
    fl, af = flux_of(qloc), flux_of(acc)
    n = acc[0]
    s_d_rows = [acc[1 + d] - qloc[1 + d] * n for d in range(3)]
    inv = 0.5 / (1.0 + n)
    rates = []
    for r in range(8):
        central = acc[30 + r]
        for d in range(3):
            central = central + fl[d][r] * s_d_rows[d] - qloc[1 + d] * af[d][r]
        if r == 7:
            central = ch * ch * central
        dissip = qloc[20] * (acc[4 + r] - qloc[4 + r] * n) + acc[12 + r] - qloc[4 + r] * acc[20]
        rates.append((dissip - central) * inv)
    nloc[0] = n
    nloc[1] = inv
    nloc[2] = dt
    rho_o[...] = qloc[4] + dt * rates[0]
    psi_o[...] = (qloc[11] + dt * rates[7]) * jnp.exp(-DAMPING * dt * ch)
    for d in range(3):
        pk[16 * d : 16 * (d + 1), :] = qloc[5 + d] + dt * rates[1 + d]
        y = qloc[8 + d] + dt * rates[4 + d]
        yz[d] = y
        prev[d] = y
        older[d] = y
        lz[d] = zero
    for j in range(BLOCKS):
        mom_o[:, TILE * j : TILE * (j + 1)] = pk[pl.ds(j, 3, stride=16), :]
    qdl[pl.ds(7, 16, stride=8), :] = zero

    table = rkl_table(SECTIONS)

    def dsplit(v):
        hi = v.astype(BF16).astype(F32)
        return jnp.concatenate([hi, v - hi], axis=0).astype(BF16)

    def section(k, c):
        def coef(m):
            val = jnp.asarray(table[0][m], F32)
            for j in range(1, SECTIONS):
                val = jnp.where(k == j, jnp.asarray(table[j][m], F32), val)
            return val

        mu, nu, c0, mut, gam = (coef(m) for m in range(5))
        y = [prev[d] for d in range(3)]
        eta = ohm_r[...] + facs[...] * (y[0] * y[0] + y[1] * y[1] + y[2] * y[2])
        for r, v in enumerate([*y, *[eta * u for u in y], eta]):
            qdl[pl.ds(r, 16, stride=8), :] = v
        got = gathered(lambda s: qdl[pl.ds(pl.multiple_of(8 * s, 8), 8), :])
        for m, v in enumerate(shifted(got)):
            dsend[k, m] = v
        cps = copies(dsend.at[k], drecv.at[k], s_d.at[k], r_d.at[k])
        for cp in cps:
            cp.start()
        for j in range(BLOCKS):
            qdb[j] = dsplit(qdl[8 * j : 8 * j + 8, :])
        for cp in cps:
            cp.wait_recv()
        for m, v in enumerate(combined(lambda m: drecv[k, m])):
            qdb[BLOCKS + m] = dsplit(v)

        def tile(t, run):
            q = qdb[tab[64 + t]]
            part = jnp.dot(jnp.concatenate([q, q], axis=1), wst[t], preferred_element_type=F32)
            run = fold(run, part[:8] + part[8:], tab[128 + t])
            accd[t] = run
            return run

        unrolled(tile, TILES, jnp.zeros((8, TILE), F32), 8)
        for i in range(BLOCKS):
            acdt[8 * i : 8 * (i + 1), :] = accd[tab[192 + i]]
        acc = [acdt[pl.ds(r, 16, stride=8), :] for r in range(7)]
        n, inv, dt = nloc[0], nloc[1], nloc[2]
        for d in range(3):
            rate = (eta * (acc[d] - y[d] * n) + acc[3 + d] - y[d] * acc[6]) * inv
            lzero = jnp.where(k == 0, rate, lz[d])
            lz[d] = lzero
            nxt = mu * y[d] + nu * older[d] + c0 * yz[d] + dt * (mut * rate + gam * lzero)
            older[d] = y[d]
            prev[d] = nxt
        for cp in cps:
            cp.wait_send()
        return c

    lax.fori_loop(0, SECTIONS, section, 0)
    for d in range(3):
        pk[16 * d : 16 * (d + 1), :] = prev[d]
    for j in range(BLOCKS):
        bfl_o[:, TILE * j : TILE * (j + 1)] = pk[pl.ds(j, 3, stride=16), :]
    for c in pay_copies:
        c.wait_send()


def tile_table(tile_i, tile_j, tile_count):
    order = jnp.arange(TILES, dtype=jnp.int32)
    used = order < tile_count[0]
    key = jnp.where(used, tile_i * 32 + tile_j, 1024 + order)
    rank = jnp.sum((key[None, :] < key[:, None]).astype(jnp.int32), axis=1)
    put = rank[:, None] == order[None, :]
    skey = jnp.sum(jnp.where(put, key[:, None], 0), axis=0)
    before = jnp.sum(jnp.where(put, 0, 0), axis=0)
    valid = skey < 1024
    si = jnp.where(valid, skey >> 5, 0)
    sj = jnp.where(valid, skey & 31, 0)
    prior = jnp.concatenate([jnp.full((1,), -1, jnp.int32), si[:-1]])
    same = (si == prior).astype(jnp.int32) + before
    blocks = jnp.arange(BLOCKS, dtype=jnp.int32)
    mine = used[None, :] & (tile_i[None, :] == blocks[:, None])
    upto = used[None, :] & (tile_i[None, :] <= blocks[:, None])
    total = jnp.sum(mine.astype(jnp.int32), axis=1)
    last = jnp.where(total > 0, jnp.sum(upto.astype(jnp.int32), axis=1) - 1, TILES)
    return jnp.concatenate([si, sj, same, last, jnp.zeros((48,), jnp.int32)])


def shards(
    positions, density, momentum, field, psi, ohmic, ambipolar, ghost_index, tile_i, tile_j, tile_count
):
    table = tile_table(tile_i, tile_j, tile_count)
    gi = jnp.concatenate([ghost_index, jnp.zeros((2048 - 1088,), jnp.int32)]).reshape(16, TILE)

    def two(v):
        return v.reshape(BLOCKS, TILE)

    vmem = pl.BlockSpec(memory_space=pltpu.VMEM)
    V = pltpu.VMEM
    D = pltpu.SemaphoreType.DMA
    out = pl.pallas_call(
        kernel,
        out_shape=(
            jax.ShapeDtypeStruct((BLOCKS, TILE), F32),
            jax.ShapeDtypeStruct((3, 2048), F32),
            jax.ShapeDtypeStruct((3, 2048), F32),
            jax.ShapeDtypeStruct((BLOCKS, TILE), F32),
        ),
        in_specs=[pl.BlockSpec(memory_space=pltpu.SMEM)] + [vmem] * 8,
        out_specs=(vmem,) * 4,
        scratch_shapes=[
            V((144, TILE), F32),
            V((GBLOCKS, 8, TILE), jnp.int32),
            V((GBLOCKS, 8, TILE), jnp.int32),
            V((256, TILE), F32),
            V((NPIECE, 16, TILE), F32),
            V((NPIECE, 16, TILE), F32),
            V((256, TILE), F32),
            V((QROWS, BLOCKS, TILE), F32),
            V((32 * QROWS, TILE), F32),
            V((25, 2 * QROWS, TILE), BF16),
            V((25, 8, TILE), F32),
            V((25, TILE, 8), F32),
            V((TILES, 2 * TILE, TILE), BF16),
            V((TILES + 1, QROWS, TILE), F32),
            V((BLOCKS * QROWS, TILE), F32),
            V((BLOCKS * 8, TILE), F32),
            V((SECTIONS, NPIECE, 8, TILE), F32),
            V((SECTIONS, NPIECE, 8, TILE), F32),
            V((25, 16, TILE), BF16),
            V((TILES + 1, 8, TILE), F32),
            V((BLOCKS * 8, TILE), F32),
            V((3, BLOCKS, TILE), F32),
            V((3, BLOCKS, TILE), F32),
            V((3, BLOCKS, TILE), F32),
            V((3, BLOCKS, TILE), F32),
            V((3, BLOCKS, TILE), F32),
            V((BLOCKS, TILE), F32),
            V((BLOCKS, TILE), F32),
            V((3, 1, TILE), F32),
            V((16, 1, TILE), F32),
            V((8, 1, TILE), F32),
            V((4, 1, TILE), F32),
            D((8,)), D((8,)), D((SECTIONS, 8)), D((SECTIONS, 8)),
            D((16,)), D((16,)), D((8,)), D((8,)), D((4,)), D((4,)),
        ],
        compiler_params=pltpu.CompilerParams(
            collective_id=0, has_side_effects=True, vmem_limit_bytes=40 * 1024 * 1024
        ),
    )(table, positions, two(density), momentum, field, two(psi), two(ohmic), two(ambipolar), gi)
    return out[0].reshape(-1), out[1], out[2], out[3].reshape(-1)


def solution(mesh):
    one, three = P(("gx", "gy")), P(None, ("gx", "gy"))
    return jax.shard_map(
        shards,
        mesh=mesh,
        in_specs=(three, one, three, three, one, one, one, one, one, one, one),
        out_specs=(one, three, three, one),
        check_vma=False,
    )
```

time: 308 us -> 74.9 us (0.24)
  the two profiles are of different devices: /device:TPU:55 before, /device:TPU:1 now
where the time goes in v1:
time: 74.9 us; the launch traced here: 74.5 us
  Pallas kernels  65.8 us (88%)
  local copies, waits for them, and re-layouts  5.46 us (7%)
  other arithmetic  1.83 us (2%)
  between operations  1.35 us (2%)
    pallas_call x1, Pallas kernels, shards(): pl.pallas_call(kernel, out_shape=(jax.ShapeDtypeStruct((BLOCKS, TILE), F3...  65.8 us
    unnamed x18, local copies, waits for them, and re-layouts  4.65 us

profile of v1, /device:TPU:1, one launch (start us, length us, event | category | flops | bytes accessed | tf_op | source)
XLA Modules:
  0.0 74.5 jit_solution(17291100909641904188)
XLA Ops:
  0.6 0.0 copy-start
  1.3 0.7 add_select_fusion
  2.0 0.2 convert_reduce_fusion
  2.1 0.1 select_reduce_fusion
  2.3 0.8 %convert_reduce_fusion.1 = (s32[16]{0:T(128)S(1)}, s32[16]{0:T(128)S(1)}) fusion(s32[64]{0:T(128)} %param.19, pred[64]{0:T(512)(128)(4,1)S(1)} %iota_compare_fusion.3), kind=kLoop, calls=%fused_computation.4 | loop fusion | flops 8160 | bytes 448 | tf_op jit(solution)/shard_map/reduce_sum | solution.py:440
  3.1 0.0 copy-start.5
  3.1 0.1 compare_convert_fusion
  3.2 0.1 concatenate.10.tab
  3.2 0.0 copy-start.3
  3.2 0.0 copy-start.4
  3.2 0.7 pad_bitcast_fusion.gi_r
  4.0 0.0 copy-done
  4.0 0.0 copy-done.5
  4.0 0.0 copy-done.3
  4.0 0.0 copy-done.4
  4.0 0.0 copy-start.1
  4.0 0.7 %copy-done.1 = f32[3,2048]{1,0:T(4,128)S(1)} copy-done((f32[3,2048]{1,0:T(4,128)S(1)}, f32[3,2048]{1,0:T(4,128)}, u32[]{:S(2)}) %copy-start.1) | copy-done | bytes 24600
  4.7 0.0 copy-start.2
  4.7 0.8 %copy-done.2 = f32[3,2048]{1,0:T(4,128)S(1)} copy-done((f32[3,2048]{1,0:T(4,128)S(1)}, f32[3,2048]{1,0:T(4,128)}, u32[]{:S(2)}) %copy-start.2) | copy-done | bytes 24600
  5.5 0.0 copy-start.6
  5.5 0.7 copy-done.6
  6.2 65.8 %shard_map.138 = (f32[16,128]{1,0:T(8,128)S(1)}, f32[3,2048]{1,0:T(4,128)S(1)}, f32[3,2048]{1,0:T(4,128)S(1)}, f32[16,128]{1,0:T(8,128)S(1)}) custom-call(s32[256]{0:T(256)S(1)} %concatenate.10.tab, f32[3,2048]{1,0:T(4,128)S(1)} %copy-done, f32[16,128]{1,0:T(8,128)S(1)} %bitcast.12, f32[3,2048]{1,0:T(4,128)S(1)} %copy-done.1, f32[3,2048]{1,0:T(4,128)S(1)} %copy-done.2, ...), custom_call_target="tpu_custom_call" | custom-call | tf_op jit(solution)/shard_map/pallas_call | solution.py:456
  72.0 0.6 copy.20
  72.7 0.6 copy.21
  73.3 0.6 copy.22
  73.9 0.6 copy.23
  (4 shorter events, 0.0 us)
Async XLA Ops:
  0.6 3.3 %copy-start = (f32[3,2048]{1,0:T(4,128)S(1)}, f32[3,2048]{1,0:T(4,128)}, u32[]{:S(2)}) copy-start(f32[3,2048]{1,0:T(4,128)} %pos.1) | copy-start | bytes 73732
  3.1 0.9 %copy-start.5 = (f32[2048]{0:T(1024)S(1)}, f32[2048]{0:T(1024)}, u32[]{:S(2)}) copy-start(f32[2048]{0:T(1024)} %param.16) | copy-start | bytes 24580
  3.2 0.7 copy-start.3
  3.2 0.7 copy-start.4
  4.0 0.8 %copy-start.1 = (f32[3,2048]{1,0:T(4,128)S(1)}, f32[3,2048]{1,0:T(4,128)}, u32[]{:S(2)}) copy-start(f32[3,2048]{1,0:T(4,128)} %mom_r.1) | copy-start | bytes 73732
  4.7 0.8 %copy-start.2 = (f32[3,2048]{1,0:T(4,128)S(1)}, f32[3,2048]{1,0:T(4,128)}, u32[]{:S(2)}) copy-start(f32[3,2048]{1,0:T(4,128)} %bfl_r.1) | copy-start | bytes 73732
  5.5 0.7 copy-start.6

commit v2 on v1

--- a/solution.py
+++ b/solution.py
@@ -82,12 +82,13 @@
 
 
 def kernel(
-    tab, pos, rho_r, mom_r, bfl_r, psi_r, ohm_r, amb_r, gi_r,
+    pos_h, rho_h, mom_h, bfl_h, psi_h, ohm_h, amb_h, gi_h, ti_h, tj_h, cnt_h,
     rho_o, mom_o, bfl_o, psi_o,
-    pk, lane_b, blk_b, pay, paysend, payrecv, ghp, qp, qt, qb, xn, xt, wst, acch, acct,
-    qdl, dsend, drecv, qdb, accd, acdt, yz, prev, older, lz, nloc, etas, facs,
+    pos_r, rho_r, mom_r, bfl_r, psi_r, ohm_r, amb_r, gi_r, gis_r, ti_r, tj_r, cnt_r, tabv, tab,
+    pk, lane_b, blk_b, pay, paysend, payrecv, ghp, qp, qt, qb, xn, xb, wst, acch, acct,
+    gsrc, qdl, dsend, drecv, qdb, accd, acdt, yz, older, lz, nloc, facs,
     mxs, mxa, mxb, mxc,
-    s_pay, r_pay, s_d, r_d, s_a, r_a, s_b, r_b, s_c, r_c,
+    s_in, s_tab, s_pay, r_pay, s_d, r_d, s_a, r_a, s_b, r_b, s_c, r_c,
 ):
     ix, iy = lax.axis_index("gx"), lax.axis_index("gy")
     xx, xy = ix // 8, ix % 8
@@ -103,6 +104,16 @@
 
     def dev_c(k):
         return (((xx + k) % 4) * 8 + xy, iy)
+
+    loads = {}
+    for n, (name, src, dst) in enumerate([
+        ("bfl", bfl_h, bfl_r), ("rho", rho_h, rho_r), ("pos", pos_h, pos_r), ("mom", mom_h, mom_r),
+        ("psi", psi_h, psi_r), ("ohm", ohm_h, ohm_r), ("amb", amb_h, amb_r),
+        ("gi", gi_h.at[pl.ds(0, 1024)], gi_r), ("gis", gi_h.at[pl.ds(1024, 64)], gis_r),
+        ("ti", ti_h, ti_r), ("tj", tj_h, tj_r), ("cnt", cnt_h, cnt_r),
+    ]):
+        loads[name] = pltpu.make_async_copy(src, dst, s_in.at[n])
+        loads[name].start()
 
     barrier = pltpu.get_barrier_semaphore()
 
@@ -120,27 +131,23 @@
         if p:
             pl.semaphore_signal(barrier, inc=1, device_id=near(p, q), device_id_type=MESH)
 
-    for j in range(BLOCKS):
-        for n, ref in enumerate((pos, mom_r, bfl_r)):
+    def pack(n, ref):
+        for j in range(BLOCKS):
             pk[pl.ds(48 * n + j, 3, stride=16), :] = ref[:, TILE * j : TILE * (j + 1)]
-
-    def packed(n):
-        return pk[16 * n : 16 * (n + 1), :]
+        return [pk[48 * n + 16 * d : 48 * n + 16 * (d + 1), :] for d in range(3)]
+
+    def unpack(n, ref):
+        for j in range(BLOCKS):
+            ref[:, TILE * j : TILE * (j + 1)] = pk[pl.ds(48 * n + j, 3, stride=16), :]
 
     ixf = ix.astype(F32)
     iyf = iy.astype(F32)
+    loads["bfl"].wait()
+    loads["rho"].wait()
     rho = rho_r[...]
-    x = [packed(0), packed(1), packed(2)]
-    mom = [packed(3), packed(4), packed(5)]
-    bfl = [packed(6), packed(7), packed(8)]
-    psi = psi_r[...]
+    bfl = pack(2, bfl_r)
     speed = jnp.sqrt(1.0 + (bfl[0] * bfl[0] + bfl[1] * bfl[1] + bfl[2] * bfl[2]) / rho)
-    facs[...] = amb_r[...] / (rho * jnp.sqrt(rho))
     mxs[0] = jnp.max(speed, axis=0, keepdims=True)
-    live = jnp.ones_like(rho)
-    zero = jnp.zeros_like(rho)
-    for r, v in enumerate([*x, live, rho, *mom, *bfl, psi, speed, zero, zero, zero]):
-        pay[pl.ds(r, 16, stride=16), :] = v
 
     pl.semaphore_wait(barrier, 15 + 7 + 3 + 6)
 
@@ -170,24 +177,57 @@
     send_c, wait_c = ring(dev_c, 4, 2, mxc, s_c, r_c)
     send_a()
 
-    gi = gi_r[...]
+    for name in ("pos", "mom", "psi", "ohm", "amb", "gi", "gis", "ti", "tj", "cnt"):
+        loads[name].wait()
+    x = pack(0, pos_r)
+    mom = pack(1, mom_r)
+    psi = psi_r[...]
+    fac = amb_r[...] / (rho * jnp.sqrt(rho))
+    facs[...] = fac
+    live = jnp.ones_like(rho)
+    zero = jnp.zeros_like(rho)
+    for r, v in enumerate([*bfl, live, *mom, rho, *x, psi, speed, ohm_r[...], fac, zero]):
+        pay[pl.ds(r, 16, stride=16), :] = v
+
+    lanes = lax.broadcasted_iota(jnp.int32, (8, TILE), 1)
+
+    def vector_of(scalar, n):
+        v = jnp.zeros((8, TILE), jnp.int32)
+        for m in range(n):
+            v = jnp.where(lanes == m, scalar(m), v)
+        return v
+
     for o in range(GBLOCKS):
-        row = jnp.broadcast_to(gi[o : o + 1, :], (8, TILE))
+        if o < 8:
+            row = jnp.broadcast_to(gi_r[TILE * o : TILE * (o + 1)].reshape(1, TILE), (8, TILE))
+        else:
+            row = vector_of(lambda m: gis_r[m], 64)
         lane_b[o] = row & 127
         blk_b[o] = row >> 7
 
-    lanes = lax.broadcasted_iota(jnp.int32, (8, TILE), 1)
-
     def gathered(load):
-        def body(s, got):
+        got = [jnp.zeros((8, TILE), F32) for _ in range(GBLOCKS)]
+        for s in range(BLOCKS):
             src = load(s)
-            new = []
             for o in range(GBLOCKS):
                 val = jnp.take_along_axis(src, lane_b[o], axis=1, mode="promise_in_bounds")
-                new.append(jnp.where(blk_b[o] == s, val, got[o]))
-            return tuple(new)
-
-        return lax.fori_loop(0, BLOCKS, body, tuple(jnp.zeros((8, TILE), F32) for _ in range(GBLOCKS)))
+                got[o] = jnp.where(blk_b[o] == s, val, got[o])
+        return got
+
+    upper = lax.broadcasted_iota(jnp.int32, (8, TILE), 0) < 4
+
+    def gathered4(rows):
+        for r, v in enumerate(rows):
+            gsrc[pl.ds(r, 8, stride=8), :] = v[:8]
+            gsrc[pl.ds(4 + r, 8, stride=8), :] = v[8:]
+        half = jnp.where(upper, 0, 8)
+        got = [jnp.zeros((8, TILE), F32) for _ in range(GBLOCKS)]
+        for o in range(GBLOCKS):
+            lane, blk = lane_b[o], blk_b[o] - half
+            for s in range(8):
+                val = jnp.take_along_axis(gsrc[8 * s : 8 * s + 8, :], lane, axis=1, mode="promise_in_bounds")
+                got[o] = jnp.where(blk == s, val, got[o])
+        return [v + pltpu.roll(v, 4, 0) for v in got]
 
     def shifted(got):
         out = []
@@ -233,13 +273,16 @@
         return out
 
     for g in range(2):
-        got = gathered(lambda s, g=g: pay[pl.ds(pl.multiple_of(16 * s + 8 * g, 8), 8), :])
+        got = gathered(lambda s, g=g: pay[16 * s + 8 * g : 16 * s + 8 * g + 8, :])
         for n, v in enumerate(shifted(got)):
             paysend[n, 8 * g : 8 * (g + 1), :] = v
     pay_copies = copies(paysend, payrecv, s_pay, r_pay)
     for c in pay_copies:
         c.start()
 
+    mxs[1] = wait_a()
+    send_b()
+
     def put_q(rows, base):
         for r, v in enumerate(rows):
             qt[pl.ds(base * QROWS + r, 16, stride=QROWS), :] = v
@@ -249,13 +292,12 @@
         qp[r] = v
     put_q([*qloc, zero, zero], 0)
 
-    mxs[1] = wait_a()
-    send_b()
-
     def put_x(j):
         tile = qt[pl.ds(pl.multiple_of(j * QROWS, 8), 8), :]
         xn[j] = tile
-        xt[j] = jnp.transpose(tile)
+        col = jnp.transpose(tile)
+        for d in range(3):
+            xb[j, d] = jnp.broadcast_to(col[:, 1 + d : 2 + d], (TILE, TILE))
 
     def split(j):
         v = qt[pl.ds(pl.multiple_of(j * QROWS, 8), QROWS), :]
@@ -268,6 +310,31 @@
         return c
 
     lax.fori_loop(0, BLOCKS, prep, 0)
+
+    row8 = (8, TILE)
+    lane = lax.broadcasted_iota(jnp.int32, row8, 1)
+    used = lane < jnp.minimum(cnt_r[0], TILES)
+    pair = vector_of(lambda m: ti_r[m] * 32 + tj_r[m], TILES)
+    key = jnp.where(used, pair, 1024 + lane)
+    keycol = jnp.broadcast_to(jnp.transpose(key)[:, 0:1], (TILE, TILE))
+    keyrow = jnp.broadcast_to(key[0:1, :], (TILE, TILE))
+    rank = jnp.sum(jnp.where(keycol < keyrow, 1, 0), axis=0, keepdims=True)
+    rank = jnp.broadcast_to(jnp.transpose(jnp.broadcast_to(rank, row8))[:, 0:1], (TILE, TILE))
+    lanes2 = lax.broadcasted_iota(jnp.int32, (TILE, TILE), 1)
+    skey = jnp.sum(jnp.where(rank == lanes2, keycol, 0), axis=0, keepdims=True)
+    total = jnp.sum(jnp.where(keycol < (lanes2 + 1) * 32, 1, 0), axis=0, keepdims=True)
+    below = jnp.sum(jnp.where(keycol < lanes2 * 32, 1, 0), axis=0, keepdims=True)
+    last = jnp.where(total > below, total - 1, TILES)
+    skey = jnp.broadcast_to(skey, row8)
+    valid = skey < 1024
+    si = jnp.where(valid, skey >> 5, 0)
+    sj = jnp.where(valid, skey & 31, 0)
+    same = jnp.where((lane > 0) & (si == pltpu.roll(si, 1, 1)), 1, 0)
+    sub = lax.broadcasted_iota(jnp.int32, row8, 0)
+    tabv[...] = jnp.where(sub == 0, si, jnp.where(sub == 1, sj, jnp.where(sub == 2, same, last)))
+    to_smem = pltpu.make_async_copy(tabv, tab, s_tab)
+    to_smem.start()
+
     mxs[2] = wait_b()
     send_c()
 
@@ -279,23 +346,26 @@
             ghp[16 * k + 8 * g : 16 * k + 8 * g + 8, :] = v
     gh = [ghp[pl.ds(r, 16, stride=16), :] for r in range(13)]
     glive = gh[3]
-    grho = jnp.where(glive > 0.0, gh[4], 1.0)
+    grho = jnp.where(glive > 0.0, gh[7], 1.0)
     gq = q_rows(
-        [glive * (gh[0] - ixf), glive * (gh[1] - iyf), gh[2]], glive, grho, gh[5:8], gh[8:11], gh[11], gh[12]
+        [glive * (gh[8] - ixf), glive * (gh[9] - iyf), gh[10]], glive, grho, gh[4:7], gh[0:3], gh[11], gh[12]
     )
     gq = [jnp.where(glive > 0.0, v, 0.0) for v in gq]
     put_q([*gq, zero, zero], BLOCKS)
     lax.fori_loop(BLOCKS, BLOCKS + GBLOCKS, prep, 0)
 
+    def inside(index, n):
+        return jnp.minimum(jnp.maximum(index, 0), n - 1)
+
     def fold(run, part, same):
         return part + jnp.where(same == 1, run, 0.0)
 
     def hydro_tile(t, run):
-        i, j = tab[t], tab[64 + t]
-        a, b = xn[i], xt[j]
-        d0 = a[1:2, :] - b[:, 1:2]
-        d1 = a[2:3, :] - b[:, 2:3]
-        d2 = a[3:4, :] - b[:, 3:4]
+        i, j = inside(tab[0, t], BLOCKS), inside(tab[1, t], BLOCKS + GBLOCKS)
+        a = xn[i]
+        d0 = a[1:2, :] - xb[j, 0]
+        d1 = a[2:3, :] - xb[j, 1]
+        d2 = a[3:4, :] - xb[j, 2]
         base = jnp.maximum(1.0 - 4.0 * (d0 * d0 + d1 * d1 + d2 * d2), 0.0)
         w = base * base
         hi = w.astype(BF16)
@@ -304,7 +374,7 @@
         wst[t] = w2
         q = qb[j]
         part = jnp.dot(jnp.concatenate([q, q], axis=1), w2, preferred_element_type=F32)
-        run = fold(run, part[:QROWS] + part[QROWS:], tab[128 + t])
+        run = fold(run, part[:QROWS] + part[QROWS:], tab[2, t])
         acch[t] = run
         return run
 
@@ -316,15 +386,12 @@
 
         return lax.fori_loop(0, n // by, step, start)
 
+    to_smem.wait()
     acch[TILES] = jnp.zeros((QROWS, TILE), F32)
     accd[TILES] = jnp.zeros((8, TILE), F32)
     unrolled(hydro_tile, TILES, jnp.zeros((QROWS, TILE), F32), 4)
     for i in range(BLOCKS):
-        acct[QROWS * i : QROWS * (i + 1), :] = acch[tab[192 + i]]
-
-    chm = jnp.max(wait_c(), axis=1, keepdims=True)
-    ch = jnp.broadcast_to(chm, (BLOCKS, TILE))
-    dt = COURANT / ch
+        acct[QROWS * i : QROWS * (i + 1), :] = acch[inside(tab[3, i], TILES + 1)]
 
     acc = [acct[pl.ds(r, 16, stride=QROWS), :] for r in range(38)]
     qloc = [qp[r] for r in range(38)]
@@ -338,132 +405,161 @@
         for d in range(3):
             central = central + fl[d][r] * s_d_rows[d] - qloc[1 + d] * af[d][r]
         if r == 7:
-            central = ch * ch * central
+            psi_central = central
+            central = 0.0
         dissip = qloc[20] * (acc[4 + r] - qloc[4 + r] * n) + acc[12 + r] - qloc[4 + r] * acc[20]
         rates.append((dissip - central) * inv)
-    nloc[0] = n
-    nloc[1] = inv
-    nloc[2] = dt
-    rho_o[...] = qloc[4] + dt * rates[0]
-    psi_o[...] = (qloc[11] + dt * rates[7]) * jnp.exp(-DAMPING * dt * ch)
-    for d in range(3):
-        pk[16 * d : 16 * (d + 1), :] = qloc[5 + d] + dt * rates[1 + d]
-        y = qloc[8 + d] + dt * rates[4 + d]
-        yz[d] = y
-        prev[d] = y
-        older[d] = y
-        lz[d] = zero
-    for j in range(BLOCKS):
-        mom_o[:, TILE * j : TILE * (j + 1)] = pk[pl.ds(j, 3, stride=16), :]
-    qdl[pl.ds(7, 16, stride=8), :] = zero
-
-    table = rkl_table(SECTIONS)
-
-    def dsplit(v):
-        hi = v.astype(BF16).astype(F32)
-        return jnp.concatenate([hi, v - hi], axis=0).astype(BF16)
-
-    def section(k, c):
-        def coef(m):
-            val = jnp.asarray(table[0][m], F32)
-            for j in range(1, SECTIONS):
-                val = jnp.where(k == j, jnp.asarray(table[j][m], F32), val)
-            return val
-
-        mu, nu, c0, mut, gam = (coef(m) for m in range(5))
-        y = [prev[d] for d in range(3)]
-        eta = ohm_r[...] + facs[...] * (y[0] * y[0] + y[1] * y[1] + y[2] * y[2])
-        for r, v in enumerate([*y, *[eta * u for u in y], eta]):
-            qdl[pl.ds(r, 16, stride=8), :] = v
-        got = gathered(lambda s: qdl[pl.ds(pl.multiple_of(8 * s, 8), 8), :])
-        for m, v in enumerate(shifted(got)):
+
+    sub = lax.broadcasted_iota(jnp.int32, (8, TILE), 0)
+
+    def exchange(k, rows):
+        for m, v in enumerate(shifted(gathered4(rows))):
             dsend[k, m] = v
         cps = copies(dsend.at[k], drecv.at[k], s_d.at[k], r_d.at[k])
         for cp in cps:
             cp.start()
+        return cps
+
+    def dsplit(v):
+        hi = v.astype(BF16).astype(F32)
+        return jnp.concatenate([hi, v - hi], axis=0).astype(BF16)
+
+    def put_local(y, eta):
+        for r, v in enumerate([*y, eta, *[eta * u for u in y], zero]):
+            qdl[pl.ds(r, 16, stride=8), :] = v
         for j in range(BLOCKS):
             qdb[j] = dsplit(qdl[8 * j : 8 * j + 8, :])
-        for cp in cps:
+
+    def put_ghost(m, v):
+        eta = jnp.broadcast_to(v[3:4, :], (8, TILE))
+        qdb[BLOCKS + m] = dsplit(v * jnp.where(upper, 1.0, jnp.where(sub < 7, eta, 0.0)))
+
+    cps = exchange(0, [*rates[4:7], zero])
+
+    chm = jnp.max(wait_c(), axis=1, keepdims=True)
+    ch = jnp.broadcast_to(chm, (BLOCKS, TILE))
+    dt = COURANT / ch
+    dt8 = dt[:8]
+    rho_o[...] = qloc[4] + dt * rates[0]
+    psi_o[...] = (qloc[11] + dt * (rates[7] - ch * ch * psi_central * inv)) * jnp.exp(-DAMPING * dt * ch)
+    for d in range(3):
+        mom_o[16 * d : 16 * (d + 1), :] = qloc[5 + d] + dt * rates[1 + d]
+        yz[d] = qloc[8 + d] + dt * rates[4 + d]
+    nloc[0] = n
+    nloc[1] = inv
+    nloc[2] = dt
+    table = rkl_table(SECTIONS)
+
+    def eta_of(y):
+        return ohm_r[...] + facs[...] * (y[0] * y[0] + y[1] * y[1] + y[2] * y[2])
+
+    def fold_tiles():
+        def tile(t, run):
+            q = qdb[inside(tab[1, t], BLOCKS + GBLOCKS)]
+            part = jnp.dot(jnp.concatenate([q, q], axis=1), wst[t], preferred_element_type=F32)
+            run = fold(run, part[:8] + part[8:], tab[2, t])
+            accd[t] = run
+            return run
+
+        unrolled(tile, TILES, jnp.zeros((8, TILE), F32), 16)
+        for i in range(BLOCKS):
+            acdt[8 * i : 8 * (i + 1), :] = accd[inside(tab[3, i], TILES + 1)]
+        return [acdt[pl.ds(r, 16, stride=8), :] for r in range(7)]
+
+    def rates_of(y, eta):
+        acc = fold_tiles()
+        n, inv = nloc[0], nloc[1]
+        return [(eta * (acc[d] - y[d] * n) + acc[4 + d] - y[d] * acc[3]) * inv for d in range(3)]
+
+    y = [yz[d] for d in range(3)]
+    eta = eta_of(y)
+    put_local(y, eta)
+    for cp in cps:
+        cp.wait_recv()
+    for m, v in enumerate(combined(lambda m: drecv[0, m])):
+        g0, g1 = ghp[16 * m : 16 * m + 8, :], ghp[16 * m + 8 : 16 * m + 16, :]
+        y0 = jnp.where(sub < 3, g0 + dt8 * v, 0.0)
+        sq = jnp.sum(y0 * y0, axis=0, keepdims=True)
+        geta = g1[5:6, :] + g1[6:7, :] * sq
+        w = jnp.where(sub == 3, jnp.broadcast_to(geta, (8, TILE)), y0)
+        put_ghost(m, w + pltpu.roll(w, 4, 0))
+    rate = rates_of(y, eta)
+    mut = table[0][3]
+    for d in range(3):
+        lz[d] = rate[d]
+        older[d] = y[d]
+    y = [y[d] + mut * dt * rate[d] for d in range(3)]
+
+    for k in range(1, SECTIONS):
+        mu, nu, c0, mut, gam = table[k]
+        eta = eta_of(y)
+        cps += exchange(k, [*y, eta])
+        put_local(y, eta)
+        base = [mu * y[d] + nu * older[d] + c0 * yz[d] + gam * dt * lz[d] for d in range(3)]
+        for d in range(3):
+            older[d] = y[d]
+        for cp in cps[8 * k :]:
             cp.wait_recv()
         for m, v in enumerate(combined(lambda m: drecv[k, m])):
-            qdb[BLOCKS + m] = dsplit(v)
-
-        def tile(t, run):
-            q = qdb[tab[64 + t]]
-            part = jnp.dot(jnp.concatenate([q, q], axis=1), wst[t], preferred_element_type=F32)
-            run = fold(run, part[:8] + part[8:], tab[128 + t])
-            accd[t] = run
-            return run
-
-        unrolled(tile, TILES, jnp.zeros((8, TILE), F32), 8)
-        for i in range(BLOCKS):
-            acdt[8 * i : 8 * (i + 1), :] = accd[tab[192 + i]]
-        acc = [acdt[pl.ds(r, 16, stride=8), :] for r in range(7)]
-        n, inv, dt = nloc[0], nloc[1], nloc[2]
-        for d in range(3):
-            rate = (eta * (acc[d] - y[d] * n) + acc[3 + d] - y[d] * acc[6]) * inv
-            lzero = jnp.where(k == 0, rate, lz[d])
-            lz[d] = lzero
-            nxt = mu * y[d] + nu * older[d] + c0 * yz[d] + dt * (mut * rate + gam * lzero)
-            older[d] = y[d]
-            prev[d] = nxt
-        for cp in cps:
-            cp.wait_send()
-        return c
-
-    lax.fori_loop(0, SECTIONS, section, 0)
+            put_ghost(m, v)
+        rate = rates_of(y, eta)
+        y = [base[d] + mut * dt * rate[d] for d in range(3)]
+
     for d in range(3):
-        pk[16 * d : 16 * (d + 1), :] = prev[d]
-    for j in range(BLOCKS):
-        bfl_o[:, TILE * j : TILE * (j + 1)] = pk[pl.ds(j, 3, stride=16), :]
-    for c in pay_copies:
+        bfl_o[16 * d : 16 * (d + 1), :] = y[d]
+    for c in pay_copies + cps:
         c.wait_send()
 
 
-def tile_table(tile_i, tile_j, tile_count):
-    order = jnp.arange(TILES, dtype=jnp.int32)
-    used = order < tile_count[0]
-    key = jnp.where(used, tile_i * 32 + tile_j, 1024 + order)
-    rank = jnp.sum((key[None, :] < key[:, None]).astype(jnp.int32), axis=1)
-    put = rank[:, None] == order[None, :]
-    skey = jnp.sum(jnp.where(put, key[:, None], 0), axis=0)
-    before = jnp.sum(jnp.where(put, 0, 0), axis=0)
-    valid = skey < 1024
-    si = jnp.where(valid, skey >> 5, 0)
-    sj = jnp.where(valid, skey & 31, 0)
-    prior = jnp.concatenate([jnp.full((1,), -1, jnp.int32), si[:-1]])
-    same = (si == prior).astype(jnp.int32) + before
-    blocks = jnp.arange(BLOCKS, dtype=jnp.int32)
-    mine = used[None, :] & (tile_i[None, :] == blocks[:, None])
-    upto = used[None, :] & (tile_i[None, :] <= blocks[:, None])
-    total = jnp.sum(mine.astype(jnp.int32), axis=1)
-    last = jnp.where(total > 0, jnp.sum(upto.astype(jnp.int32), axis=1) - 1, TILES)
-    return jnp.concatenate([si, sj, same, last, jnp.zeros((48,), jnp.int32)])
+def finish(rho_p, mom_p, bfl_p, psi_p, rho_h, mom_h, bfl_h, psi_h, mom_r, bfl_r, sems):
+    first = [
+        pltpu.make_async_copy(rho_p, rho_h, sems.at[0]),
+        pltpu.make_async_copy(psi_p, psi_h, sems.at[1]),
+    ]
+    for c in first:
+        c.start()
+    for src, dst in ((mom_p, mom_r), (bfl_p, bfl_r)):
+        for j in range(BLOCKS):
+            dst[:, TILE * j : TILE * (j + 1)] = src[pl.ds(j, 3, stride=16), :]
+    second = [
+        pltpu.make_async_copy(mom_r, mom_h, sems.at[2]),
+        pltpu.make_async_copy(bfl_r, bfl_h, sems.at[3]),
+    ]
+    for c in second:
+        c.start()
+    for c in first + second:
+        c.wait()
 
 
 def shards(
     positions, density, momentum, field, psi, ohmic, ambipolar, ghost_index, tile_i, tile_j, tile_count
 ):
-    table = tile_table(tile_i, tile_j, tile_count)
-    gi = jnp.concatenate([ghost_index, jnp.zeros((2048 - 1088,), jnp.int32)]).reshape(16, TILE)
+    def pin(v):
+        return pltpu.with_memory_space_constraint(v, pltpu.HBM) if v.shape[0] != 1 else v
 
     def two(v):
         return v.reshape(BLOCKS, TILE)
 
     vmem = pl.BlockSpec(memory_space=pltpu.VMEM)
+    hbm = pl.BlockSpec(memory_space=pltpu.HBM)
     V = pltpu.VMEM
+    I32 = jnp.int32
     D = pltpu.SemaphoreType.DMA
     out = pl.pallas_call(
         kernel,
         out_shape=(
             jax.ShapeDtypeStruct((BLOCKS, TILE), F32),
-            jax.ShapeDtypeStruct((3, 2048), F32),
-            jax.ShapeDtypeStruct((3, 2048), F32),
+            jax.ShapeDtypeStruct((48, TILE), F32),
+            jax.ShapeDtypeStruct((48, TILE), F32),
             jax.ShapeDtypeStruct((BLOCKS, TILE), F32),
         ),
-        in_specs=[pl.BlockSpec(memory_space=pltpu.SMEM)] + [vmem] * 8,
+        in_specs=[hbm] * 11,
         out_specs=(vmem,) * 4,
         scratch_shapes=[
+            V((3, 2048), F32), V((16, TILE), F32), V((3, 2048), F32), V((3, 2048), F32),
+            V((16, TILE), F32), V((16, TILE), F32), V((16, TILE), F32),
+            V((1024,), I32), pltpu.SMEM((64,), I32), pltpu.SMEM((64,), I32), pltpu.SMEM((64,), I32), pltpu.SMEM((1,), I32),
+            V((8, TILE), I32), pltpu.SMEM((8, TILE), I32),
             V((144, TILE), F32),
             V((GBLOCKS, 8, TILE), jnp.int32),
             V((GBLOCKS, 8, TILE), jnp.int32),
@@ -475,10 +571,11 @@
             V((32 * QROWS, TILE), F32),
             V((25, 2 * QROWS, TILE), BF16),
             V((25, 8, TILE), F32),
-            V((25, TILE, 8), F32),
+            V((25, 3, TILE, TILE), F32),
             V((TILES, 2 * TILE, TILE), BF16),
             V((TILES + 1, QROWS, TILE), F32),
             V((BLOCKS * QROWS, TILE), F32),
+            V((64, TILE), F32),
             V((BLOCKS * 8, TILE), F32),
             V((SECTIONS, NPIECE, 8, TILE), F32),
             V((SECTIONS, NPIECE, 8, TILE), F32),
@@ -489,20 +586,34 @@
             V((3, BLOCKS, TILE), F32),
             V((3, BLOCKS, TILE), F32),
             V((3, BLOCKS, TILE), F32),
-            V((3, BLOCKS, TILE), F32),
-            V((BLOCKS, TILE), F32),
             V((BLOCKS, TILE), F32),
             V((3, 1, TILE), F32),
             V((16, 1, TILE), F32),
             V((8, 1, TILE), F32),
             V((4, 1, TILE), F32),
-            D((8,)), D((8,)), D((SECTIONS, 8)), D((SECTIONS, 8)),
+            D((12,)), D, D((8,)), D((8,)), D((SECTIONS, 8)), D((SECTIONS, 8)),
             D((16,)), D((16,)), D((8,)), D((8,)), D((4,)), D((4,)),
         ],
         compiler_params=pltpu.CompilerParams(
-            collective_id=0, has_side_effects=True, vmem_limit_bytes=40 * 1024 * 1024
+            collective_id=0, has_side_effects=True, vmem_limit_bytes=48 * 1024 * 1024
         ),
-    )(table, positions, two(density), momentum, field, two(psi), two(ohmic), two(ambipolar), gi)
+    )(*map(pin, [
+        positions, two(density), momentum, field, two(psi), two(ohmic), two(ambipolar),
+        ghost_index, tile_i, tile_j, tile_count,
+    ]))
+    out = pl.pallas_call(
+        finish,
+        out_shape=(
+            jax.ShapeDtypeStruct((BLOCKS, TILE), F32),
+            jax.ShapeDtypeStruct((3, 2048), F32),
+            jax.ShapeDtypeStruct((3, 2048), F32),
+            jax.ShapeDtypeStruct((BLOCKS, TILE), F32),
+        ),
+        in_specs=[vmem] * 4,
+        out_specs=(hbm,) * 4,
+        scratch_shapes=[V((3, 2048), F32), V((3, 2048), F32), D((4,))],
+        compiler_params=pltpu.CompilerParams(vmem_limit_bytes=1024 * 1024),
+    )(*out)
     return out[0].reshape(-1), out[1], out[2], out[3].reshape(-1)
 
 

time: 74.9 us -> 59 us (0.79)
  Pallas kernels: 65.8 us -> 57.5 us
  local copies, waits for them, and re-layouts: 5.46 us -> 0 us
  other arithmetic: 1.83 us -> 0 us
    pallas_call x1, Pallas kernels: 65.8 us -> 56.8 us  [shards(): pl.pallas_call(kernel, out_shape=(jax.ShapeDtypeStruct((BLOCKS, TILE), F3...]
    unnamed x18 -> x0, local copies, waits for them, and re-layouts: 4.65 us -> none
    reduce_sum x3 -> x0, other arithmetic: 1.06 us -> none  [the longest x1 0.77 us: tile_table(): jnp.sum(upto.astype(jnp.int32), axis=1) - 1]
where the time goes in v2:
time: 59 us; the launch traced here: 58.8 us
  Pallas kernels  57.5 us (97%)
  between operations  1.29 us (2%)
    pallas_call x1, Pallas kernels, shards(): pl.pallas_call(kernel, out_shape=(jax.ShapeDtypeStruct((BLOCKS, TILE), F3...  56.8 us

profile of v2, /device:TPU:1, one launch (start us, length us, event | category | flops | bytes accessed | tf_op | source)
XLA Modules:
  0.0 58.8 jit_solution(13193121972668654859)
XLA Ops:
  1.3 56.8 %shard_map.138 = (f32[16,128]{1,0:T(8,128)S(1)}, f32[48,128]{1,0:T(8,128)S(1)}, f32[48,128]{1,0:T(8,128)S(1)}, f32[16,128]{1,0:T(8,128)S(1)}) custom-call(f32[3,2048]{1,0:T(4,128)} %pos_h.1, f32[16,128]{1,0:T(8,128)} %bitcast.6, f32[3,2048]{1,0:T(4,128)} %mom_h.1, f32[3,2048]{1,0:T(4,128)} %bfl_h.1, f32[16,128]{1,0:T(8,128)} %bitcast.7, f32[16,128]{1,0:T(8,128)} %bitcast.8, ...), custom_call_target="tpu_custom_call" | custom-call | tf_op jit(solution)/shard_map/pallas_call | solution.py:548
  58.1 0.7 %shard_map.139 = (f32[16,128]{1,0:T(8,128)}, f32[3,2048]{1,0:T(4,128)}, f32[3,2048]{1,0:T(4,128)}, f32[16,128]{1,0:T(8,128)}) custom-call(f32[16,128]{1,0:T(8,128)S(1)} %get-tuple-element.12.rho_p, f32[48,128]{1,0:T(8,128)S(1)} %get-tuple-element.13.mom_p, f32[48,128]{1,0:T(8,128)S(1)} %get-tuple-element.14.bfl_p, f32[16,128]{1,0:T(8,128)S(1)} %get-tuple-element.15.psi_p), custom_call_target="tpu_custom_call" | custom-call | tf_op jit(solution)/shard_map/pallas_call | solution.py:604

commit v3 on v2

--- a/solution.py
+++ b/solution.py
@@ -31,6 +31,8 @@
 NPIECE = len(PIECES)
 
 QROWS = 40
+CORNER_PIECES = sorted((lo, k, n) for n, (d, k, lo, hi) in enumerate(PIECES) if all(DIRECTIONS[d]))
+CORNERS = [BLOCKS + k for lo, k, n in CORNER_PIECES]
 
 
 def rkl_table(sections):
@@ -85,7 +87,7 @@
     pos_h, rho_h, mom_h, bfl_h, psi_h, ohm_h, amb_h, gi_h, ti_h, tj_h, cnt_h,
     rho_o, mom_o, bfl_o, psi_o,
     pos_r, rho_r, mom_r, bfl_r, psi_r, ohm_r, amb_r, gi_r, gis_r, ti_r, tj_r, cnt_r, tabv, tab,
-    pk, lane_b, blk_b, pay, paysend, payrecv, ghp, qp, qt, qb, xn, xb, wst, acch, acct,
+    pk, lane_b, blk_b, pay, paysend, payrecv, ghp, qp, qt, qb, xn, xb, wst, wcor, acch, acct,
     gsrc, qdl, dsend, drecv, qdb, accd, acdt, yz, older, lz, nloc, facs,
     mxs, mxa, mxb, mxc,
     s_in, s_tab, s_pay, r_pay, s_d, r_d, s_a, r_a, s_b, r_b, s_c, r_c,
@@ -149,7 +151,6 @@
     speed = jnp.sqrt(1.0 + (bfl[0] * bfl[0] + bfl[1] * bfl[1] + bfl[2] * bfl[2]) / rho)
     mxs[0] = jnp.max(speed, axis=0, keepdims=True)
 
-    pl.semaphore_wait(barrier, 15 + 7 + 3 + 6)
 
     def ring(dev, n, src, dst, ss, rs):
         def one(k):
@@ -175,7 +176,6 @@
     send_a, wait_a = ring(dev_a, 16, 0, mxa, s_a, r_a)
     send_b, wait_b = ring(dev_b, 8, 1, mxb, s_b, r_b)
     send_c, wait_c = ring(dev_c, 4, 2, mxc, s_c, r_c)
-    send_a()
 
     for name in ("pos", "mom", "psi", "ohm", "amb", "gi", "gis", "ti", "tj", "cnt"):
         loads[name].wait()
@@ -249,12 +249,12 @@
         e = (ix + p >= 0) & (ix + p < 32) & (iy + q >= 0) & (iy + q < 16)
         exists.append(e)
 
-    def combined(load):
+    def combined(load, corners):
         out = []
-        for k in range(GBLOCKS):
+        for k in range(1 if corners else GBLOCKS):
             tile = jnp.zeros((8, TILE), F32)
             for n, (d, kk, lo, hi) in enumerate(PIECES):
-                if kk == k:
+                if corners if all(DIRECTIONS[d]) and corners is not None else kk == k and not corners:
                     mask = (lanes >= lo) & (lanes < hi) & exists[d]
                     tile = jnp.where(mask, load(n), tile)
             out.append(tile)
@@ -276,12 +276,11 @@
         got = gathered(lambda s, g=g: pay[16 * s + 8 * g : 16 * s + 8 * g + 8, :])
         for n, v in enumerate(shifted(got)):
             paysend[n, 8 * g : 8 * (g + 1), :] = v
+    pl.semaphore_wait(barrier, 15 + 7 + 3 + 6)
+    send_a()
     pay_copies = copies(paysend, payrecv, s_pay, r_pay)
     for c in pay_copies:
         c.start()
-
-    mxs[1] = wait_a()
-    send_b()
 
     def put_q(rows, base):
         for r, v in enumerate(rows):
@@ -294,6 +293,7 @@
 
     def put_x(j):
         tile = qt[pl.ds(pl.multiple_of(j * QROWS, 8), 8), :]
+        tile = tile * 2.0
         xn[j] = tile
         col = jnp.transpose(tile)
         for d in range(3):
@@ -331,17 +331,27 @@
     sj = jnp.where(valid, skey & 31, 0)
     same = jnp.where((lane > 0) & (si == pltpu.roll(si, 1, 1)), 1, 0)
     sub = lax.broadcasted_iota(jnp.int32, row8, 0)
-    tabv[...] = jnp.where(sub == 0, si, jnp.where(sub == 1, sj, jnp.where(sub == 2, same, last)))
+    want = (lane >> 2) * 32 + jnp.where(
+        lane % 4 == 0, CORNERS[0], jnp.where(lane % 4 == 1, CORNERS[1], jnp.where(lane % 4 == 2, CORNERS[2], CORNERS[3]))
+    )
+    skeycol = jnp.broadcast_to(jnp.transpose(skey)[:, 0:1], (TILE, TILE))
+    hit = skeycol == jnp.broadcast_to(want[0:1, :], (TILE, TILE))
+    place = lax.broadcasted_iota(jnp.int32, (TILE, TILE), 0)
+    corner = TILES + jnp.sum(jnp.where(hit, place - TILES, 0), axis=0, keepdims=True)
+    corner = jnp.broadcast_to(corner, row8)
+    tabv[...] = jnp.where(
+        sub == 0, si, jnp.where(sub == 1, sj, jnp.where(sub == 2, same, jnp.where(sub == 3, last, corner)))
+    )
     to_smem = pltpu.make_async_copy(tabv, tab, s_tab)
     to_smem.start()
 
-    mxs[2] = wait_b()
-    send_c()
+    mxs[1] = wait_a()
+    send_b()
 
     for c in pay_copies:
         c.wait_recv()
     for g in range(2):
-        tiles = combined(lambda n, g=g: payrecv[n, 8 * g : 8 * (g + 1), :])
+        tiles = combined(lambda n, g=g: payrecv[n, 8 * g : 8 * (g + 1), :], None)
         for k, v in enumerate(tiles):
             ghp[16 * k + 8 * g : 16 * k + 8 * g + 8, :] = v
     gh = [ghp[pl.ds(r, 16, stride=16), :] for r in range(13)]
@@ -366,7 +376,7 @@
         d0 = a[1:2, :] - xb[j, 0]
         d1 = a[2:3, :] - xb[j, 1]
         d2 = a[3:4, :] - xb[j, 2]
-        base = jnp.maximum(1.0 - 4.0 * (d0 * d0 + d1 * d1 + d2 * d2), 0.0)
+        base = jnp.maximum(1.0 - (d0 * d0 + d1 * d1 + d2 * d2), 0.0)
         w = base * base
         hi = w.astype(BF16)
         lo = (w - hi.astype(F32)).astype(BF16)
@@ -378,18 +388,23 @@
         acch[t] = run
         return run
 
-    def unrolled(body, n, start, by):
+    def unrolled(body, first, end, start, by):
         def step(s, c):
             for u in range(by):
                 c = body(s * by + u, c)
             return c
 
-        return lax.fori_loop(0, n // by, step, start)
+        return lax.fori_loop(first // by, end // by, step, start)
 
     to_smem.wait()
     acch[TILES] = jnp.zeros((QROWS, TILE), F32)
     accd[TILES] = jnp.zeros((8, TILE), F32)
-    unrolled(hydro_tile, TILES, jnp.zeros((QROWS, TILE), F32), 4)
+    run = unrolled(hydro_tile, 0, TILES // 2, jnp.zeros((QROWS, TILE), F32), 4)
+    mxs[2] = wait_b()
+    send_c()
+    unrolled(hydro_tile, TILES // 2, TILES, run, 4)
+    wst[TILES] = jnp.zeros((2 * TILE, TILE), BF16)
+
     for i in range(BLOCKS):
         acct[QROWS * i : QROWS * (i + 1), :] = acch[inside(tab[3, i], TILES + 1)]
 
@@ -430,11 +445,21 @@
         for j in range(BLOCKS):
             qdb[j] = dsplit(qdl[8 * j : 8 * j + 8, :])
 
-    def put_ghost(m, v):
+    def ghost_rows(v):
         eta = jnp.broadcast_to(v[3:4, :], (8, TILE))
-        qdb[BLOCKS + m] = dsplit(v * jnp.where(upper, 1.0, jnp.where(sub < 7, eta, 0.0)))
+        return dsplit(v * jnp.where(upper, 1.0, jnp.where(sub < 7, eta, 0.0)))
 
     cps = exchange(0, [*rates[4:7], zero])
+
+    def corner_weights(i, c):
+        for m in range(4):
+            s = inside(tab[4, 4 * i + m], TILES + 1)
+            for h in range(2):
+                rows = pl.ds(TILE * h + 32 * m, 32)
+                wcor[i, rows, :] = wst[s, rows, :]
+        return c
+
+    lax.fori_loop(0, BLOCKS, corner_weights, 0)
 
     chm = jnp.max(wait_c(), axis=1, keepdims=True)
     ch = jnp.broadcast_to(chm, (BLOCKS, TILE))
@@ -453,7 +478,7 @@
     def eta_of(y):
         return ohm_r[...] + facs[...] * (y[0] * y[0] + y[1] * y[1] + y[2] * y[2])
 
-    def fold_tiles():
+    def fold_tiles(corner):
         def tile(t, run):
             q = qdb[inside(tab[1, t], BLOCKS + GBLOCKS)]
             part = jnp.dot(jnp.concatenate([q, q], axis=1), wst[t], preferred_element_type=F32)
@@ -461,29 +486,59 @@
             accd[t] = run
             return run
 
-        unrolled(tile, TILES, jnp.zeros((8, TILE), F32), 16)
+        unrolled(tile, 0, TILES, jnp.zeros((8, TILE), F32), 16)
+        q = corner()
+        q2 = jnp.concatenate([q, q], axis=1)
         for i in range(BLOCKS):
-            acdt[8 * i : 8 * (i + 1), :] = accd[inside(tab[3, i], TILES + 1)]
+            part = jnp.dot(q2, wcor[i], preferred_element_type=F32)
+            acdt[8 * i : 8 * (i + 1), :] = accd[inside(tab[3, i], TILES + 1)] + (part[:8] + part[8:])
         return [acdt[pl.ds(r, 16, stride=8), :] for r in range(7)]
 
-    def rates_of(y, eta):
-        acc = fold_tiles()
+    def rates_of(y, eta, corner):
+        acc = fold_tiles(corner)
         n, inv = nloc[0], nloc[1]
         return [(eta * (acc[d] - y[d] * n) + acc[4 + d] - y[d] * acc[3]) * inv for d in range(3)]
 
     y = [yz[d] for d in range(3)]
     eta = eta_of(y)
     put_local(y, eta)
-    for cp in cps:
-        cp.wait_recv()
-    for m, v in enumerate(combined(lambda m: drecv[0, m])):
-        g0, g1 = ghp[16 * m : 16 * m + 8, :], ghp[16 * m + 8 : 16 * m + 16, :]
+    straight = [d for d in range(8) if not all(DIRECTIONS[d])]
+    diagonal = [d for d in range(8) if all(DIRECTIONS[d])]
+
+    def start_rows(g0, g1, v):
         y0 = jnp.where(sub < 3, g0 + dt8 * v, 0.0)
         sq = jnp.sum(y0 * y0, axis=0, keepdims=True)
         geta = g1[5:6, :] + g1[6:7, :] * sq
         w = jnp.where(sub == 3, jnp.broadcast_to(geta, (8, TILE)), y0)
-        put_ghost(m, w + pltpu.roll(w, 4, 0))
-    rate = rates_of(y, eta)
+        return ghost_rows(w + pltpu.roll(w, 4, 0))
+
+    def payload_tile(m, g):
+        return ghp[16 * m + 8 * g : 16 * m + 8 * g + 8, :]
+
+    def keep(tile, m):
+        for lo, k, n in CORNER_PIECES:
+            if k == m:
+                tile = jnp.where((lanes >= lo) & (lanes < lo + 32), 0.0, tile)
+        return tile
+
+    def corner_payload(g):
+        tile = payload_tile(CORNER_PIECES[0][1], g)
+        for lo, k, n in CORNER_PIECES[1:]:
+            tile = jnp.where(lanes >= lo, payload_tile(k, g), tile)
+        return tile
+
+    for d in straight:
+        cps[d].wait_recv()
+    for m, v in enumerate(combined(lambda m: drecv[0, m], False)):
+        qdb[BLOCKS + m] = start_rows(keep(payload_tile(m, 0), m), keep(payload_tile(m, 1), m), v)
+
+    def corner_start():
+        for d in diagonal:
+            cps[d].wait_recv()
+        [v] = combined(lambda m: drecv[0, m], True)
+        return start_rows(corner_payload(0), corner_payload(1), v)
+
+    rate = rates_of(y, eta, corner_start)
     mut = table[0][3]
     for d in range(3):
         lz[d] = rate[d]
@@ -498,11 +553,18 @@
         base = [mu * y[d] + nu * older[d] + c0 * yz[d] + gam * dt * lz[d] for d in range(3)]
         for d in range(3):
             older[d] = y[d]
-        for cp in cps[8 * k :]:
-            cp.wait_recv()
-        for m, v in enumerate(combined(lambda m: drecv[k, m])):
-            put_ghost(m, v)
-        rate = rates_of(y, eta)
+        for d in straight:
+            cps[8 * k + d].wait_recv()
+        for m, v in enumerate(combined(lambda m, k=k: drecv[k, m], False)):
+            qdb[BLOCKS + m] = ghost_rows(v)
+
+        def corner_next(k=k):
+            for d in diagonal:
+                cps[8 * k + d].wait_recv()
+            [v] = combined(lambda m: drecv[k, m], True)
+            return ghost_rows(v)
+
+        rate = rates_of(y, eta, corner_next)
         y = [base[d] + mut * dt * rate[d] for d in range(3)]
 
     for d in range(3):
@@ -572,7 +634,8 @@
             V((25, 2 * QROWS, TILE), BF16),
             V((25, 8, TILE), F32),
             V((25, 3, TILE, TILE), F32),
-            V((TILES, 2 * TILE, TILE), BF16),
+            V((TILES + 1, 2 * TILE, TILE), BF16),
+            V((BLOCKS, 2 * TILE, TILE), BF16),
             V((TILES + 1, QROWS, TILE), F32),
             V((BLOCKS * QROWS, TILE), F32),
             V((64, TILE), F32),

time: 59 us -> 54.6 us (0.925)
  Pallas kernels: 57.5 us -> 53.1 us
    pallas_call x1, Pallas kernels: 56.8 us -> 52.4 us  [shards(): pl.pallas_call(kernel, out_shape=(jax.ShapeDtypeStruct((BLOCKS, TILE), F3...]
where the time goes in v3:
time: 54.6 us; the launch traced here: 54.4 us
  Pallas kernels  53.1 us (97%)
  between operations  1.29 us (2%)
    pallas_call x1, Pallas kernels, shards(): pl.pallas_call(kernel, out_shape=(jax.ShapeDtypeStruct((BLOCKS, TILE), F3...  52.4 us

profile of v3, /device:TPU:1, one launch (start us, length us, event | category | flops | bytes accessed | tf_op | source)
XLA Modules:
  0.0 54.4 jit_solution(18255547473914274177)
XLA Ops:
  1.3 52.4 %shard_map.138 = (f32[16,128]{1,0:T(8,128)S(1)}, f32[48,128]{1,0:T(8,128)S(1)}, f32[48,128]{1,0:T(8,128)S(1)}, f32[16,128]{1,0:T(8,128)S(1)}) custom-call(f32[3,2048]{1,0:T(4,128)} %pos_h.1, f32[16,128]{1,0:T(8,128)} %bitcast.6, f32[3,2048]{1,0:T(4,128)} %mom_h.1, f32[3,2048]{1,0:T(4,128)} %bfl_h.1, f32[16,128]{1,0:T(8,128)} %bitcast.7, f32[16,128]{1,0:T(8,128)} %bitcast.8, ...), custom_call_target="tpu_custom_call" | custom-call | tf_op jit(solution)/shard_map/pallas_call | solution.py:610
  53.7 0.7 %shard_map.139 = (f32[16,128]{1,0:T(8,128)}, f32[3,2048]{1,0:T(4,128)}, f32[3,2048]{1,0:T(4,128)}, f32[16,128]{1,0:T(8,128)}) custom-call(f32[16,128]{1,0:T(8,128)S(1)} %get-tuple-element.12.rho_p, f32[48,128]{1,0:T(8,128)S(1)} %get-tuple-element.13.mom_p, f32[48,128]{1,0:T(8,128)S(1)} %get-tuple-element.14.bfl_p, f32[16,128]{1,0:T(8,128)S(1)} %get-tuple-element.15.psi_p), custom_call_target="tpu_custom_call" | custom-call | tf_op jit(solution)/shard_map/pallas_call | solution.py:667

commit v4 on v3

--- a/solution.py
+++ b/solution.py
@@ -29,6 +29,9 @@
         PIECES.append((d, k, lo, hi))
 COUNT = [sum(1 for p in PIECES if p[0] == d) for d in range(8)]
 NPIECE = len(PIECES)
+
+STRAIGHT = [d for d in range(8) if not all(DIRECTIONS[d])]
+DIAGONAL = [d for d in range(8) if all(DIRECTIONS[d])]
 
 QROWS = 40
 CORNER_PIECES = sorted((lo, k, n) for n, (d, k, lo, hi) in enumerate(PIECES) if all(DIRECTIONS[d]))
@@ -177,6 +180,8 @@
     send_b, wait_b = ring(dev_b, 8, 1, mxb, s_b, r_b)
     send_c, wait_c = ring(dev_c, 4, 2, mxc, s_c, r_c)
 
+    pl.semaphore_wait(barrier, 15 + 7 + 3 + 6)
+    send_a()
     for name in ("pos", "mom", "psi", "ohm", "amb", "gi", "gis", "ti", "tj", "cnt"):
         loads[name].wait()
     x = pack(0, pos_r)
@@ -216,33 +221,27 @@
 
     upper = lax.broadcasted_iota(jnp.int32, (8, TILE), 0) < 4
 
-    def gathered4(rows):
-        for r, v in enumerate(rows):
-            gsrc[pl.ds(r, 8, stride=8), :] = v[:8]
-            gsrc[pl.ds(4 + r, 8, stride=8), :] = v[8:]
-        half = jnp.where(upper, 0, 8)
-        got = [jnp.zeros((8, TILE), F32) for _ in range(GBLOCKS)]
-        for o in range(GBLOCKS):
-            lane, blk = lane_b[o], blk_b[o] - half
-            for s in range(8):
-                val = jnp.take_along_axis(gsrc[8 * s : 8 * s + 8, :], lane, axis=1, mode="promise_in_bounds")
-                got[o] = jnp.where(blk == s, val, got[o])
-        return [v + pltpu.roll(v, 4, 0) for v in got]
-
-    def shifted(got):
-        out = []
-        for d, k, lo, hi in PIECES:
-            shift = STARTS[d] - STARTS[7 - d]
-            a, s = shift // TILE, shift % TILE
-            if lo >= s:
-                out.append(pltpu.roll(got[k - a], s, 1) if s else got[k - a])
-            elif hi <= s:
-                out.append(pltpu.roll(got[k - a - 1], s, 1))
-            else:
-                out.append(
-                    jnp.where(lanes >= s, pltpu.roll(got[k - a], s, 1), pltpu.roll(got[k - a - 1], s, 1))
-                )
-        return out
+    def gathered4(o):
+        got = jnp.zeros((8, TILE), F32)
+        lane, blk = lane_b[o], blk_b[o] - jnp.where(upper, 0, 8)
+        for s in range(8):
+            val = jnp.take_along_axis(gsrc[8 * s : 8 * s + 8, :], lane, axis=1, mode="promise_in_bounds")
+            got = jnp.where(blk == s, val, got)
+        return got + pltpu.roll(got, 4, 0)
+
+    def shifted(piece, got):
+        d, k, lo, hi = piece
+        shift = STARTS[d] - STARTS[7 - d]
+        a, s = shift // TILE, shift % TILE
+
+        def turned(o):
+            return pltpu.roll(got(o), s, 1) if s else got(o)
+
+        if lo >= s:
+            return turned(k - a)
+        if hi <= s:
+            return turned(k - a - 1)
+        return jnp.where(lanes >= s, turned(k - a), turned(k - a - 1))
 
     exists = []
     for p, q in DIRECTIONS:
@@ -274,13 +273,11 @@
 
     for g in range(2):
         got = gathered(lambda s, g=g: pay[16 * s + 8 * g : 16 * s + 8 * g + 8, :])
-        for n, v in enumerate(shifted(got)):
-            paysend[n, 8 * g : 8 * (g + 1), :] = v
-    pl.semaphore_wait(barrier, 15 + 7 + 3 + 6)
-    send_a()
+        for n, piece in enumerate(PIECES):
+            paysend[n, 8 * g : 8 * (g + 1), :] = shifted(piece, lambda o: got[o])
     pay_copies = copies(paysend, payrecv, s_pay, r_pay)
-    for c in pay_copies:
-        c.start()
+    for d in DIAGONAL + STRAIGHT:
+        pay_copies[d].start()
 
     def put_q(rows, base):
         for r, v in enumerate(rows):
@@ -304,12 +301,16 @@
         hi = v.astype(BF16).astype(F32)
         qb[j] = jnp.concatenate([hi, v - hi], axis=0).astype(BF16)
 
-    def prep(j, c):
-        put_x(j)
-        split(j)
-        return c
-
-    lax.fori_loop(0, BLOCKS, prep, 0)
+    def prep(first, n, by):
+        def step(s, c):
+            for u in range(by):
+                put_x(first + s * by + u)
+                split(first + s * by + u)
+            return c
+
+        lax.fori_loop(0, n // by, step, 0)
+
+    prep(0, BLOCKS, 8)
 
     row8 = (8, TILE)
     lane = lax.broadcasted_iota(jnp.int32, row8, 1)
@@ -362,7 +363,7 @@
     )
     gq = [jnp.where(glive > 0.0, v, 0.0) for v in gq]
     put_q([*gq, zero, zero], BLOCKS)
-    lax.fori_loop(BLOCKS, BLOCKS + GBLOCKS, prep, 0)
+    prep(BLOCKS, GBLOCKS, 9)
 
     def inside(index, n):
         return jnp.minimum(jnp.maximum(index, 0), n - 1)
@@ -399,10 +400,10 @@
     to_smem.wait()
     acch[TILES] = jnp.zeros((QROWS, TILE), F32)
     accd[TILES] = jnp.zeros((8, TILE), F32)
-    run = unrolled(hydro_tile, 0, TILES // 2, jnp.zeros((QROWS, TILE), F32), 4)
+    run = unrolled(hydro_tile, 0, TILES // 2, jnp.zeros((QROWS, TILE), F32), 16)
     mxs[2] = wait_b()
     send_c()
-    unrolled(hydro_tile, TILES // 2, TILES, run, 4)
+    unrolled(hydro_tile, TILES // 2, TILES, run, 16)
     wst[TILES] = jnp.zeros((2 * TILE, TILE), BF16)
 
     for i in range(BLOCKS):
@@ -428,11 +429,23 @@
     sub = lax.broadcasted_iota(jnp.int32, (8, TILE), 0)
 
     def exchange(k, rows):
-        for m, v in enumerate(shifted(gathered4(rows))):
-            dsend[k, m] = v
+        for r, v in enumerate(rows):
+            gsrc[pl.ds(r, 8, stride=8), :] = v[:8]
+            gsrc[pl.ds(4 + r, 8, stride=8), :] = v[8:]
         cps = copies(dsend.at[k], drecv.at[k], s_d.at[k], r_d.at[k])
-        for cp in cps:
-            cp.start()
+        got = {}
+
+        def rows_of(o):
+            if o not in got:
+                got[o] = gathered4(o)
+            return got[o]
+
+        for part in (DIAGONAL, STRAIGHT):
+            for m, piece in enumerate(PIECES):
+                if piece[0] in part:
+                    dsend[k, m] = shifted(piece, rows_of)
+            for d in part:
+                cps[d].start()
         return cps
 
     def dsplit(v):
@@ -486,7 +499,7 @@
             accd[t] = run
             return run
 
-        unrolled(tile, 0, TILES, jnp.zeros((8, TILE), F32), 16)
+        unrolled(tile, 0, TILES, jnp.zeros((8, TILE), F32), 64)
         q = corner()
         q2 = jnp.concatenate([q, q], axis=1)
         for i in range(BLOCKS):
@@ -502,9 +515,6 @@
     y = [yz[d] for d in range(3)]
     eta = eta_of(y)
     put_local(y, eta)
-    straight = [d for d in range(8) if not all(DIRECTIONS[d])]
-    diagonal = [d for d in range(8) if all(DIRECTIONS[d])]
-
     def start_rows(g0, g1, v):
         y0 = jnp.where(sub < 3, g0 + dt8 * v, 0.0)
         sq = jnp.sum(y0 * y0, axis=0, keepdims=True)
@@ -527,13 +537,13 @@
             tile = jnp.where(lanes >= lo, payload_tile(k, g), tile)
         return tile
 
-    for d in straight:
+    for d in STRAIGHT:
         cps[d].wait_recv()
     for m, v in enumerate(combined(lambda m: drecv[0, m], False)):
         qdb[BLOCKS + m] = start_rows(keep(payload_tile(m, 0), m), keep(payload_tile(m, 1), m), v)
 
     def corner_start():
-        for d in diagonal:
+        for d in DIAGONAL:
             cps[d].wait_recv()
         [v] = combined(lambda m: drecv[0, m], True)
         return start_rows(corner_payload(0), corner_payload(1), v)
@@ -553,13 +563,13 @@
         base = [mu * y[d] + nu * older[d] + c0 * yz[d] + gam * dt * lz[d] for d in range(3)]
         for d in range(3):
             older[d] = y[d]
-        for d in straight:
+        for d in STRAIGHT:
             cps[8 * k + d].wait_recv()
         for m, v in enumerate(combined(lambda m, k=k: drecv[k, m], False)):
             qdb[BLOCKS + m] = ghost_rows(v)
 
         def corner_next(k=k):
-            for d in diagonal:
+            for d in DIAGONAL:
                 cps[8 * k + d].wait_recv()
             [v] = combined(lambda m: drecv[k, m], True)
             return ghost_rows(v)

time: 54.6 us -> 51.6 us (0.945)
  Pallas kernels: 53.1 us -> 50.1 us
    pallas_call x1, Pallas kernels: 52.4 us -> 49.4 us  [shards(): pl.pallas_call(kernel, out_shape=(jax.ShapeDtypeStruct((BLOCKS, TILE), F3...]
where the time goes in v4:
time: 51.6 us; the launch traced here: 51.4 us
  Pallas kernels  50.1 us (97%)
  between operations  1.29 us (2%)
    pallas_call x1, Pallas kernels, shards(): pl.pallas_call(kernel, out_shape=(jax.ShapeDtypeStruct((BLOCKS, TILE), F3...  49.4 us

profile of v4, /device:TPU:1, one launch (start us, length us, event | category | flops | bytes accessed | tf_op | source)
XLA Modules:
  0.0 51.4 jit_solution(18380404643407773752)
XLA Ops:
  1.3 49.4 %shard_map.138 = (f32[16,128]{1,0:T(8,128)S(1)}, f32[48,128]{1,0:T(8,128)S(1)}, f32[48,128]{1,0:T(8,128)S(1)}, f32[16,128]{1,0:T(8,128)S(1)}) custom-call(f32[3,2048]{1,0:T(4,128)} %pos_h.1, f32[16,128]{1,0:T(8,128)} %bitcast.6, f32[3,2048]{1,0:T(4,128)} %mom_h.1, f32[3,2048]{1,0:T(4,128)} %bfl_h.1, f32[16,128]{1,0:T(8,128)} %bitcast.7, f32[16,128]{1,0:T(8,128)} %bitcast.8, ...), custom_call_target="tpu_custom_call" | custom-call | tf_op jit(solution)/shard_map/pallas_call | solution.py:620
  50.7 0.7 %shard_map.139 = (f32[16,128]{1,0:T(8,128)}, f32[3,2048]{1,0:T(4,128)}, f32[3,2048]{1,0:T(4,128)}, f32[16,128]{1,0:T(8,128)}) custom-call(f32[16,128]{1,0:T(8,128)S(1)} %get-tuple-element.12.rho_p, f32[48,128]{1,0:T(8,128)S(1)} %get-tuple-element.13.mom_p, f32[48,128]{1,0:T(8,128)S(1)} %get-tuple-element.14.bfl_p, f32[16,128]{1,0:T(8,128)S(1)} %get-tuple-element.15.psi_p), custom_call_target="tpu_custom_call" | custom-call | tf_op jit(solution)/shard_map/pallas_call | solution.py:677

commit v5 on v4

--- a/solution.py
+++ b/solution.py
@@ -400,10 +400,10 @@
     to_smem.wait()
     acch[TILES] = jnp.zeros((QROWS, TILE), F32)
     accd[TILES] = jnp.zeros((8, TILE), F32)
-    run = unrolled(hydro_tile, 0, TILES // 2, jnp.zeros((QROWS, TILE), F32), 16)
+    run = unrolled(hydro_tile, 0, TILES // 2, jnp.zeros((QROWS, TILE), F32), 32)
     mxs[2] = wait_b()
     send_c()
-    unrolled(hydro_tile, TILES // 2, TILES, run, 16)
+    unrolled(hydro_tile, TILES // 2, TILES, run, 32)
     wst[TILES] = jnp.zeros((2 * TILE, TILE), BF16)
 
     for i in range(BLOCKS):

time: 51.6 us -> 51.5 us (level)
  no operation moved by 1% of the time
where the time goes in v5:
time: 51.5 us; the launch traced here: 51.3 us
  Pallas kernels  50 us (97%)
  between operations  1.29 us (3%)
    pallas_call x1, Pallas kernels, shards(): pl.pallas_call(kernel, out_shape=(jax.ShapeDtypeStruct((BLOCKS, TILE), F3...  49.3 us

profile of v5, /device:TPU:1, one launch (start us, length us, event | category | flops | bytes accessed | tf_op | source)
XLA Modules:
  0.0 51.3 jit_solution(5392149957752102231)
XLA Ops:
  1.3 49.3 %shard_map.138 = (f32[16,128]{1,0:T(8,128)S(1)}, f32[48,128]{1,0:T(8,128)S(1)}, f32[48,128]{1,0:T(8,128)S(1)}, f32[16,128]{1,0:T(8,128)S(1)}) custom-call(f32[3,2048]{1,0:T(4,128)} %pos_h.1, f32[16,128]{1,0:T(8,128)} %bitcast.6, f32[3,2048]{1,0:T(4,128)} %mom_h.1, f32[3,2048]{1,0:T(4,128)} %bfl_h.1, f32[16,128]{1,0:T(8,128)} %bitcast.7, f32[16,128]{1,0:T(8,128)} %bitcast.8, ...), custom_call_target="tpu_custom_call" | custom-call | tf_op jit(solution)/shard_map/pallas_call | solution.py:620
  50.6 0.7 %shard_map.139 = (f32[16,128]{1,0:T(8,128)}, f32[3,2048]{1,0:T(4,128)}, f32[3,2048]{1,0:T(4,128)}, f32[16,128]{1,0:T(8,128)}) custom-call(f32[16,128]{1,0:T(8,128)S(1)} %get-tuple-element.12.rho_p, f32[48,128]{1,0:T(8,128)S(1)} %get-tuple-element.13.mom_p, f32[48,128]{1,0:T(8,128)S(1)} %get-tuple-element.14.bfl_p, f32[16,128]{1,0:T(8,128)S(1)} %get-tuple-element.15.psi_p), custom_call_target="tpu_custom_call" | custom-call | tf_op jit(solution)/shard_map/pallas_call | solution.py:677
